TPU v7x, 32 devices: a whole 2x2x4 slice. The times are simulated.
32 devices in a mesh: groups: 2 (over y), fsdp: 4 (over z), replica: 4 (over x, core).
Axes of the slice: x: 2, y: 2, z: 4, core: 2. Of those that a mesh axis runs over, the one named last changes fastest.
Arguments:
- hidden: bfloat16 [4, 3072, 2560], P('replica', ('groups', 'fsdp')), parts along dimension 1, may hold values from -6 to 6
- targets: int32 [4, 3072], P('replica', ('groups', 'fsdp')), parts along dimension 1, may hold values from 0 to 440
- params: float32 [4, 5120, 441], P('replica', ('groups', 'fsdp')), parts along dimension 1, may hold values from -0.875 to 0.875
- moment: float32 [4, 5120, 441], P('replica', ('groups', 'fsdp')), parts along dimension 1, may hold values from -24 to 24
- second: float32 [4, 5120, 441], P('replica', ('groups', 'fsdp')), parts along dimension 1, may hold values from 1 to 100
- train_step: int32 [1], replicated, may hold values from 1 to 99999
Outputs:
- averaged: float32 [4, 5120, 441], P('replica', ('groups', 'fsdp')), parts along dimension 1
- moment_new: float32 [4, 5120, 441], P('replica', ('groups', 'fsdp')), parts along dimension 1
- second_new: float32 [4, 5120, 441], P('replica', ('groups', 'fsdp')), parts along dimension 1
- grad_hidden: bfloat16 [4, 3072, 2560], P('replica', ('groups', 'fsdp')), parts along dimension 1
There are 2 independent parts, one for each index of `groups`. A program takes and returns all parts, laid end to end along the dimension named above; an argument that names none is the same for every part. Nothing has to cross between parts.
All inputs are finite; a program needn't handle non-finite values.
Results may differ from a plain program's by a relative error of at most 0.0049.
The roundings to bfloat16 on the way count: a program that leaves them out, or rounds other values in their place, can miss the bound.
Values may be sent and summed in bfloat16 or wider, within the bound.
No kernel may reach another device: no remote copies, remote signals or barrier semaphores. Data moves between devices by JAX's collectives and lax.ppermute only.
A program may use at most 64 MiB of HBM per device.

v0:
```python
import math

import jax
import jax.numpy as jnp
from jax import lax
from jax.sharding import PartitionSpec as P

norm_eps = 1e-05
logit_cap = 30.0
learn_rate = 0.001
weight_decay = 0.1
beta_one = 0.9
beta_two = 0.999
adam_eps = 1e-08


def shortened(x):
    return jax.tree.map(lambda a: a.astype(jnp.bfloat16) if a.dtype == jnp.float32 else a, x)


def from_partner(block, axis, stride):
    count = lax.axis_size(axis)
    route = []
    for low in range(count):
        high = low | 1 << stride
        if high != low and high < count:
            route += [(low, high), (high, low)]
    return lax.ppermute(block, axis, route)


def normalize(token_block):
    values = token_block.astype(jnp.float32)
    center = values - jnp.mean(values, axis=-1, keepdims=True)
    inv_scale = lax.rsqrt(jnp.mean(center * center, axis=-1, keepdims=True) + norm_eps)
    return (center * inv_scale, inv_scale)


def pair_with(bit_index):

    def swap_values(values):
        return jax.tree.map(
            lambda part, own: part.astype(own.dtype),
            from_partner(shortened(values), "replica", bit_index),
            values,
        )

    return swap_values


def local(hidden, targets, params, moment, second, train_step):
    normalized, inv_scale = normalize(hidden[0])
    normed_bf = normalized.astype(jnp.bfloat16)
    labels = targets[0]
    shard_bf = params[0].astype(jnp.bfloat16)
    vocab_width = shard_bf.shape[1]
    weight_bf = lax.all_gather(shard_bf, "fsdp", axis=0, tiled=True)
    raw_logits = jnp.dot(normed_bf, weight_bf, preferred_element_type=jnp.float32)
    capped = jnp.tanh(raw_logits / logit_cap)
    exp_logits = jnp.exp(logit_cap * capped)
    softmax_p = exp_logits / jnp.sum(exp_logits, axis=-1, keepdims=True)
    onehot = (labels[:, None] == jnp.arange(vocab_width, dtype=jnp.int32)[None, :]).astype(
        jnp.float32
    )
    logit_grad = ((softmax_p - onehot) * (1.0 - capped * capped)).astype(jnp.bfloat16)
    full_grad = lax.dot_general(
        normed_bf, logit_grad, (((0,), (0,)), ((), ())), preferred_element_type=jnp.float32
    )
    grad_shard = lax.psum_scatter(
        full_grad.astype(jnp.bfloat16), "fsdp", scatter_dimension=0, tiled=True
    ).astype(jnp.float32)
    normed_grad = lax.dot_general(
        logit_grad, weight_bf, (((1,), (1,)), ((), ())), preferred_element_type=jnp.float32
    )
    first_mean = jnp.mean(normed_grad, axis=-1, keepdims=True)
    second_mean = jnp.mean(normed_grad * normalized, axis=-1, keepdims=True)
    grad_hidden = (inv_scale * (normed_grad - first_mean - normalized * second_mean)).astype(
        jnp.bfloat16
    )
    tcount = train_step[0].astype(jnp.float32)
    fix_one = 1.0 - jnp.exp(tcount * math.log(beta_one))
    fix_two = 1.0 - jnp.exp(tcount * math.log(beta_two))
    replica_grads = grad_shard[None]
    moment_new = beta_one * moment + (1.0 - beta_one) * replica_grads
    second_new = beta_two * second + (1.0 - beta_two) * replica_grads * replica_grads
    adam_step = moment_new / fix_one / (jnp.sqrt(second_new / fix_two) + adam_eps)
    updated = params - learn_rate * (adam_step + weight_decay * params)
    levels = lax.axis_size("replica").bit_length() - 1
    partner_values = lax.switch(
        train_step[0] % levels, [pair_with(bit_index) for bit_index in range(levels)], updated
    )
    averaged = 0.5 * (updated + partner_values)
    return (averaged, moment_new, second_new, grad_hidden[None])


def solution(mesh):
    placed = (
        P("replica", ("groups", "fsdp"), None),
        P("replica", ("groups", "fsdp")),
        P("replica", ("groups", "fsdp"), None),
        P("replica", ("groups", "fsdp"), None),
        P("replica", ("groups", "fsdp"), None),
        P(),
    )
    return jax.shard_map(
        local,
        mesh=mesh,
        in_specs=placed,
        out_specs=(
            P("replica", ("groups", "fsdp"), None),
            P("replica", ("groups", "fsdp"), None),
            P("replica", ("groups", "fsdp"), None),
            P("replica", ("groups", "fsdp"), None),
        ),
        check_vma=False,
    )
```

profile of v0, /device:TPU:0, one launch (start us, length us, event | category | flops | bytes accessed | tf_op | source)
XLA Modules:
  0.0 182.6 jit_solution(5841978325345324)
XLA Ops:
  7.2 0.0 copy-start.3
  7.2 0.0 copy-start
  7.2 0.0 all-gather.3.cloned.1.call-start
  7.2 3.2 %convert_element_type.54 = bf16[1,640,441]{1,0,2:T(2,128)(2,1)} convert(f32[1,640,441]{1,0,2:T(1,128)} %param.10) | non-fusion elementwise | flops 282240 | bytes 1693440 | tf_op jit(solution)/shard_map/convert_element_type | solution.py:54
  10.4 0.0 all-gather.3.cloned.1.call-update
  10.4 0.0 reduce-scatter.4.cloned.1.call-start
  10.5 0.0 copy-done.3
  10.5 0.0 copy-done
  10.5 0.3 convert_reduce_fusion
  10.8 0.7 fusion.10
  11.5 87.8 %all-gather.3.cloned.1.call-done = bf16[1,2560,441]{1,0,2:T(2,128)(2,1)} async-done(((bf16[1,640,441]{1,0,2:T(2,128)(2,1)}), bf16[1,2560,441]{1,0,2:T(2,128)(2,1)}) %all-gather.3.cloned.1.call-update) | async-done | bytes 2257936 | tf_op jit(solution)/shard_map/all_gather | solution.py:56
  99.3 3.9 %fusion.28 = (f32[384]{0:T(512)S(1)}, f32[384,441]{0,1:T(8,128)S(1)}) fusion(bf16[1,2560,441]{1,0,2:T(2,128)(2,1)} %all-gather.3.cloned.1.call-done, bf16[1,384,2560]{2,1,0:T(8,128)(2,1)S(1)} %copy-done, f32[384]{0:T(512)S(1)} %add_rsqrt_fusion, f32[384]{0:T(512)S(1)} %broadcast_multiply_fusion.2), kind=kOutput, calls=%fused_computation.36 | convolution fusion | flops 871481088 | bytes 4905984 | tf_op jit(solution)/shard_map/dot_general | solution.py:57
  103.2 3.0 %convolution_convert_fusion = bf16[2560,441]{0,1:T(8,128)(2,1)} fusion(bf16[1,384,2560]{2,1,0:T(8,128)(2,1)S(1)} %copy-done, f32[384]{0:T(512)S(1)} %add_rsqrt_fusion, f32[384]{0:T(512)S(1)} %broadcast_multiply_fusion.2, f32[384,441]{0,1:T(8,128)S(1)} %get-tuple-element.29, s32[384]{0:T(512)S(1)} %reduce.1, f32[384]{0:T(512)S(1)} %get-tuple-element.28), kind=kOutput, calls=%fused_computation.2 | convolution fusion | flops 873626496 | bytes 4907520 | tf_op jit(solution)/shard_map/dot_general | solution.py:65
  106.2 4.3 %copy.27 = bf16[2560,441]{1,0:T(8,128)(2,1)} copy(bf16[2560,441]{0,1:T(8,128)(2,1)} %convolution_convert_fusion) | data formatting | bytes 4515840
  110.5 0.0 reduce-scatter.4.cloned.1.call-update
  111.3 4.3 %fusion.31 = (f32[384]{0:T(512)S(1)}, f32[384]{0:T(512)S(1)}, f32[384,2560]{1,0:T(8,128)S(1)}) fusion(f32[384]{0:T(512)S(1)} %add_rsqrt_fusion, f32[384]{0:T(512)S(1)} %broadcast_multiply_fusion.2, bf16[1,384,2560]{2,1,0:T(8,128)(2,1)S(1)} %copy-done, bf16[1,2560,441]{1,0,2:T(2,128)(2,1)} %all-gather.3.cloned.1.call-done, ...), kind=kOutput, calls=%fused_computation.41 | convolution fusion | flops 874462848 | bytes 8842752 | tf_op jit(solution)/shard_map/dot_general | solution.py:71
  115.6 2.4 %fusion.15 = bf16[1,384,2560]{2,1,0:T(8,128)(2,1)} fusion(bf16[1,384,2560]{2,1,0:T(8,128)(2,1)S(1)} %copy-done, f32[384,2560]{1,0:T(8,128)S(1)} %get-tuple-element.30, f32[384]{0:T(512)S(1)} %get-tuple-element.31, f32[384]{0:T(512)S(1)} %get-tuple-element.32, f32[384]{0:T(512)S(1)} %add_rsqrt_fusion, f32[384]{0:T(512)S(1)} %broadcast_multiply_fusion.2), kind=kLoop, calls=%fused_computation.18 | loop fusion | flops 7864320 | bytes 7870464 | tf_op jit(solution)/shard_map/broadcast_in_dim | solution.py:92
  118.0 0.0 copy-start.2
  118.0 43.0 %reduce-scatter.4.cloned.1.call-done = bf16[640,441]{1,0:T(8,128)(2,1)} async-done(((bf16[2560,441]{1,0:T(8,128)(2,1)}), bf16[640,441]{1,0:T(8,128)(2,1)}) %reduce-scatter.4.cloned.1.call-update) | async-done | bytes 564496
  161.0 2.2 %copy.28 = bf16[640,441]{0,1:T(8,128)(2,1)} copy(bf16[640,441]{1,0:T(8,128)(2,1)} %reduce-scatter.4.cloned.1.call-done) | data formatting | bytes 1128960
  163.2 0.0 copy-done.2
  163.2 3.6 %multiply_subtract_fusion = (f32[1,640,441]{1,2,0:T(8,128)S(1)}, f32[1,640,441]{1,2,0:T(8,128)S(1)}, f32[1,640,441]{1,2,0:T(8,128)}) fusion(f32[1,640,441]{1,0,2:T(1,128)S(1)} %copy-done.2, f32[]{:T(128)S(6)} %sub.49, f32[]{:T(128)S(6)} %sub.48, bf16[640,441]{0,1:T(8,128)(2,1)} %copy.28, f32[1,640,441]{1,0,2:T(1,128)} %param.12, f32[1,640,441]{1,0,2:T(1,128)} %param.11), kind=kLoop, calls=%fused_computation.30 | loop fusion | flops 4515840 | bytes 7338248 | tf_op jit(solution)/shard_map/sub | solution.py:86
  166.8 2.4 %conditional.4 = (f32[1,640,441]{1,2,0:T(8,128)S(1)}) conditional(s32[]{:T(128)} %clamp.3, f32[1,640,441]{1,2,0:T(8,128)S(1)} %get-tuple-element.25, f32[1,640,441]{1,2,0:T(8,128)S(1)} %get-tuple-element.25), branch_computations={%region_4.0_spmd, %region_5.0_spmd} | conditional | flops 564480 | bytes 5644848
  166.8 0.1 convert_element_type.36
  166.9 0.1 collective-permute-start
  166.9 2.0 %collective-permute-done = bf16[1,640,441]{1,2,0:T(8,128)(2,1)S(1)} collective-permute-done((bf16[1,640,441]{1,2,0:T(8,128)(2,1)S(1)}, bf16[1,640,441]{1,2,0:T(8,128)(2,1)S(1)}, u32[]{:S(2)}, u32[]{:S(2)}) %collective-permute-start) | collective-permute-done | bytes 564512 | tf_op jit(solution)/shard_map/cond/branch_0_fun/ppermute | solution.py:28
  168.9 0.1 convert_element_type.37
  169.2 0.1 add_multiply_fusion
  169.3 0.0 copy-start.1
  169.3 2.2 %copy.24 = f32[1,640,441]{1,0,2:T(1,128)} copy(f32[1,640,441]{1,2,0:T(8,128)S(1)} %add_multiply_fusion) | data formatting | bytes 2257920
  171.5 0.0 copy-done.1
  171.5 2.2 %copy.25 = f32[1,640,441]{1,0,2:T(1,128)} copy(f32[1,640,441]{1,2,0:T(8,128)S(1)} %copy-done.1) | data formatting | bytes 2257920
  173.6 2.2 %copy.26 = f32[1,640,441]{1,0,2:T(1,128)} copy(f32[1,640,441]{1,2,0:T(8,128)S(1)} %get-tuple-element.26) | data formatting | bytes 2257920
  (4 shorter events, 0.0 us)
Async XLA Ops:
  7.2 3.3 %copy-start.3 = (s32[1,384]{1,0:T(1,128)S(1)}, s32[1,384]{1,0:T(1,128)}, u32[]{:S(2)}) copy-start(s32[1,384]{1,0:T(1,128)} %param.9) | copy-start | bytes 4612
  7.2 3.3 %copy-start = (bf16[1,384,2560]{2,1,0:T(8,128)(2,1)S(1)}, bf16[1,384,2560]{2,1,0:T(8,128)(2,1)}, u32[]{:S(2)}) copy-start(bf16[1,384,2560]{2,1,0:T(8,128)(2,1)} %param.8) | copy-start | bytes 5898244
  7.2 92.2 %all-gather.3.cloned.1.call-start = ((), (), s32[]{:S(2)}) async-start(), calls=%async_computation.1 | async-start | bytes 5644800 | tf_op jit(solution)/shard_map/all_gather | solution.py:56
  10.4 150.6 %reduce-scatter.4.cloned.1.call-start = ((), (), s32[]{:S(2)}) async-start(), calls=%async_computation.2 | async-start | bytes 3276800
  118.0 45.2 %copy-start.2 = (f32[1,640,441]{1,0,2:T(1,128)S(1)}, f32[1,640,441]{1,0,2:T(1,128)}, u32[]{:S(2)}) copy-start(f32[1,640,441]{1,0,2:T(1,128)} %param.10) | copy-start | bytes 3386884
  166.9 2.0 %collective-permute-start = (bf16[1,640,441]{1,2,0:T(8,128)(2,1)S(1)}, bf16[1,640,441]{1,2,0:T(8,128)(2,1)S(1)}, u32[]{:S(2)}, u32[]{:S(2)}) collective-permute-start(bf16[1,640,441]{1,2,0:T(8,128)(2,1)S(1)} %convert_element_type.36), channel_id=1, source_target_pairs={{0,1},{1,0},{2,3},{3,2},{4,5},{5,4},{6,7},{7,6},{8,9},{9,8},{10,11... | collective-permute-start | bytes 1693448 | tf_op jit(solution)/shard_map/cond/branch_0_fun/ppermute | solution.py:28
  169.3 2.2 %copy-start.1 = (f32[1,640,441]{1,2,0:T(8,128)S(1)}, f32[1,640,441]{1,2,0:T(8,128)}, u32[]{:S(2)}) copy-start(f32[1,640,441]{1,2,0:T(8,128)} %get-tuple-element.27) | copy-start | bytes 3386884
Sparse Core Ops, SparseCore 0:
  10.5 88.7 all-gather.2
  110.7 50.2 reduce-scatter.3
where the time goes:
time: 183 us
  waiting for transfers between devices  133 us (73%)
  between operations  14.9 us (8%)
  local copies, waits for them, and re-layouts  13 us (7%)
  matrix products  11.1 us (6%)
  other arithmetic  10.5 us (6%)
    all_gather x1, waiting for transfers between devices, local(): weight_bf = lax.all_gather(shard_bf, 'fsdp', axis=0, tiled=True)  87.8 us
    unnamed x3, waiting for transfers between devices  43 us
    unnamed x13, local copies, waits for them, and re-layouts  13 us
    dot_general x1, matrix products, local(): lax.dot_general(logit_grad, weight_bf, (((1,), (1,)), ((), ())), preferre...  4.26 us
    dot_general x1, matrix products, local(): jnp.dot(normed_bf, weight_bf, preferred_element_type=jnp.float32)  3.86 us
  transfers between devices with their start and end apart: 3, of which 3 were waited for; matrix products, arithmetic and copies ran while one was open for 4% of the time, Pallas kernels for 0%

commit v1 on v0

--- a/solution.py
+++ b/solution.py
@@ -3,6 +3,8 @@
 import jax
 import jax.numpy as jnp
 from jax import lax
+from jax.experimental import pallas as pl
+from jax.experimental.pallas import tpu as pltpu
 from jax.sharding import PartitionSpec as P
 
 norm_eps = 1e-05
@@ -47,7 +49,7 @@
     return swap_values
 
 
-def local(hidden, targets, params, moment, second, train_step):
+def local_any(hidden, targets, params, moment, second, train_step):
     normalized, inv_scale = normalize(hidden[0])
     normed_bf = normalized.astype(jnp.bfloat16)
     labels = targets[0]
@@ -92,6 +94,302 @@
     return (averaged, moment_new, second_new, grad_hidden[None])
 
 
+near_route = [(0, 1), (1, 0), (2, 3), (3, 2)]
+far_route = [(0, 2), (2, 0), (1, 3), (3, 1)]
+mid_route = [(1, 2), (2, 1)]
+outward_route = [(1, 0), (2, 3)]
+inward_route = [(0, 1), (3, 2)]
+
+f32 = jnp.float32
+bf16 = jnp.bfloat16
+vmem = pl.BlockSpec(memory_space=pltpu.VMEM)
+smem = pl.BlockSpec(memory_space=pltpu.SMEM)
+anywhere = pl.BlockSpec(memory_space=pl.ANY)
+
+
+def shaped(shape, dtype):
+    return jax.ShapeDtypeStruct(shape, dtype)
+
+
+def run(kernel, ins, outs, args, scratch=(), limit=24, flops=0, moved=0):
+    single = not isinstance(outs, (list, tuple))
+    out_specs = vmem if single else [vmem] * len(outs)
+    return pl.pallas_call(
+        kernel,
+        in_specs=ins,
+        out_specs=out_specs,
+        out_shape=outs,
+        scratch_shapes=list(scratch),
+        compiler_params=pltpu.CompilerParams(vmem_limit_bytes=limit << 20),
+        cost_estimate=pl.CostEstimate(flops=flops, bytes_accessed=moved, transcendentals=0),
+    )(*args)
+
+
+def columns(block, width):
+    return pl.ds(pl.multiple_of(block * width, 128), width)
+
+
+def nt_dot(a, b):
+    return lax.dot_general(a, b, (((1,), (1,)), ((), ())), preferred_element_type=f32)
+
+
+def tn_dot(a, b):
+    return lax.dot_general(a, b, (((0,), (0,)), ((), ())), preferred_element_type=f32)
+
+
+def round_weight_kernel(params_ref, out_ref, held, sem):
+    vocab = held.shape[0]
+    copy = pltpu.make_async_copy(params_ref.at[:, 0, :], held, sem)
+    copy.start()
+    copy.wait()
+    out_ref[0:vocab, :] = held[...].astype(bf16)
+    out_ref[vocab:, :] = jnp.zeros((out_ref.shape[0] - vocab, out_ref.shape[1]), bf16)
+
+
+def norm_kernel(place_ref, hidden_ref, normed_ref, mean_ref, inv_ref):
+    rows, width = hidden_ref.shape
+    depth = normed_ref.shape[2]
+    step = 128
+    for top in range(0, rows, step):
+        part = pl.ds(top, step)
+        values = hidden_ref[part, :].astype(f32)
+        mean = jnp.mean(values, axis=-1, keepdims=True)
+        center = values - mean
+        inv = lax.rsqrt(jnp.mean(center * center, axis=-1, keepdims=True) + norm_eps)
+        mean_ref[part, :] = mean
+        inv_ref[part, :] = inv
+        for slot in range(normed_ref.shape[0]):
+            block = place_ref[0] ^ slot
+            own = hidden_ref[part, columns(block, depth)].astype(f32)
+            normed_ref[slot, part, :] = ((own - mean) * inv).astype(bf16)
+
+
+def partial_kernel(own_ref, near_ref, far_ref, normed_ref, acc_ref):
+    acc = nt_dot(own_ref[...], normed_ref[0])
+    acc = acc + nt_dot(near_ref[...], normed_ref[1])
+    acc_ref[...] = acc + nt_dot(far_ref[...], normed_ref[2])
+
+
+def cross_block(place_ref, mid_ref, outer_ref):
+    middle = (place_ref[0] == 1) | (place_ref[0] == 2)
+    return jnp.where(middle, mid_ref[...], outer_ref[...])
+
+
+def head_kernel(vocab, place_ref, acc_ref, mid_ref, outer_ref, normed_ref, labels_ref, lg_ref, cross_ref):
+    raw = acc_ref[...] + nt_dot(cross_block(place_ref, mid_ref, outer_ref), normed_ref[3])
+    capped = jnp.tanh(raw / logit_cap)
+    ids = lax.broadcasted_iota(jnp.int32, raw.shape, 0)
+    exp_logits = jnp.where(ids < vocab, jnp.exp(logit_cap * capped), 0.0)
+    softmax_p = exp_logits / jnp.sum(exp_logits, axis=0, keepdims=True)
+    onehot = (ids == labels_ref[...]).astype(f32)
+    logit_grad = ((softmax_p - onehot) * (1.0 - capped * capped)).astype(bf16)
+    lg_ref[...] = logit_grad
+    cross_ref[...] = jnp.dot(logit_grad, normed_ref[3], preferred_element_type=f32).astype(bf16)
+
+
+def grads_kernel(lg_ref, normed_ref, own_ref, near_ref, far_ref):
+    for slot, out in enumerate((own_ref, near_ref, far_ref)):
+        out[...] = jnp.dot(lg_ref[...], normed_ref[slot], preferred_element_type=f32).astype(bf16)
+
+
+def add_kernel(a_ref, b_ref, out_ref):
+    out_ref[...] = (a_ref[...].astype(f32) + b_ref[...].astype(f32)).astype(bf16)
+
+
+def hidden_grad_kernel(
+    place_ref, lg_ref, own_ref, near_ref, far_ref, mid_ref, outer_ref, hidden_ref, mean_ref, inv_ref, out_ref, held
+):
+    rows, width = hidden_ref.shape
+    slots, _, depth = held.shape
+    mean, inv = mean_ref[...], inv_ref[...]
+    first = jnp.zeros((rows, 1), f32)
+    second = jnp.zeros((rows, 1), f32)
+    for slot in range(slots):
+        if slot == 3:
+            block = cross_block(place_ref, mid_ref, outer_ref)
+        else:
+            block = (own_ref, near_ref, far_ref)[slot][...]
+        back = tn_dot(lg_ref[...], block)
+        held[slot] = back
+        normalized = (hidden_ref[:, columns(place_ref[0] ^ slot, depth)].astype(f32) - mean) * inv
+        first = first + jnp.sum(back, axis=-1, keepdims=True)
+        second = second + jnp.sum(back * normalized, axis=-1, keepdims=True)
+    first, second = first / width, second / width
+    for slot in range(slots):
+        part = columns(place_ref[0] ^ slot, depth)
+        normalized = (hidden_ref[:, part].astype(f32) - mean) * inv
+        out_ref[:, part] = (inv * (held[slot] - first - normalized * second)).astype(bf16)
+
+
+def summed_grads(vocab, refs):
+    return sum(ref[0:vocab, :].astype(f32) for ref in refs)
+
+
+def step_kernel(fix_ref, own_ref, near_ref, far_ref, mid_ref, params_ref, moment_ref, second_ref,
+                updated_ref, sent_ref, sems, params_in, moment_in, second_in):
+    vocab = updated_ref.shape[0]
+    copies = []
+    for slot, (src, dst) in enumerate(
+        ((moment_ref, moment_in), (second_ref, second_in), (params_ref, params_in))
+    ):
+        copies.append(pltpu.make_async_copy(src.at[:, 0, :], dst, sems.at[slot]))
+        copies[-1].start()
+    for copy in copies:
+        copy.wait()
+    grads = summed_grads(vocab, (own_ref, near_ref, far_ref, mid_ref))
+    moment_new = beta_one * moment_in[...] + (1.0 - beta_one) * grads
+    second_new = beta_two * second_in[...] + (1.0 - beta_two) * grads * grads
+    adam_step = moment_new / fix_ref[0] / (jnp.sqrt(second_new / fix_ref[1]) + adam_eps)
+    params = params_in[...]
+    updated = params - learn_rate * (adam_step + weight_decay * params)
+    updated_ref[...] = updated
+    sent_ref[0:vocab, :] = updated.astype(bf16)
+    sent_ref[vocab:, :] = jnp.zeros((sent_ref.shape[0] - vocab, sent_ref.shape[1]), bf16)
+
+
+def moments_kernel(own_ref, near_ref, far_ref, mid_ref, moment_ref, second_ref, moment_out, second_out,
+                   sems, moment_in, second_in):
+    vocab = moment_in.shape[0]
+    into = [
+        pltpu.make_async_copy(moment_ref.at[:, 0, :], moment_in, sems.at[0]),
+        pltpu.make_async_copy(second_ref.at[:, 0, :], second_in, sems.at[1]),
+    ]
+    for copy in into:
+        copy.start()
+    for copy in into:
+        copy.wait()
+    grads = summed_grads(vocab, (own_ref, near_ref, far_ref, mid_ref))
+    moment_in[...] = beta_one * moment_in[...] + (1.0 - beta_one) * grads
+    back = [pltpu.make_async_copy(moment_in, moment_out.at[:, 0, :], sems.at[0])]
+    back[0].start()
+    second_in[...] = beta_two * second_in[...] + (1.0 - beta_two) * grads * grads
+    back.append(pltpu.make_async_copy(second_in, second_out.at[:, 0, :], sems.at[1]))
+    back[1].start()
+    for copy in back:
+        copy.wait()
+
+
+def average_kernel(updated_ref, partner_ref, out_ref, sem, held):
+    vocab = held.shape[0]
+    held[...] = 0.5 * (updated_ref[...] + partner_ref[0:vocab, :].astype(f32))
+    copy = pltpu.make_async_copy(held, out_ref.at[:, 0, :], sem)
+    copy.start()
+    copy.wait()
+
+
+def by_vocab(shard):
+    return jnp.transpose(shard, (2, 0, 1))
+
+
+def local_line(hidden, targets, params, moment, second, train_step):
+    tokens, width = hidden.shape[1:]
+    depth, vocab = params.shape[1:]
+    padded = -(-vocab // 16) * 16
+    place = lax.axis_index("fsdp")[None]
+    params_t, moment_t, second_t = by_vocab(params), by_vocab(moment), by_vocab(second)
+    shard = shaped((padded, depth), bf16)
+    state = pltpu.VMEM((vocab, depth), f32)
+    state_out = shaped((vocab, 1, depth), f32)
+    dma = pltpu.SemaphoreType.DMA
+    dot_flops = 2 * padded * tokens * depth
+
+    own = run(round_weight_kernel, [anywhere], shard, (params_t,), [state, dma])
+    far = lax.ppermute(own, "fsdp", far_route)
+    near = lax.ppermute(own, "fsdp", near_route)
+    normed, mean, inv = run(
+        norm_kernel,
+        [smem, vmem],
+        [shaped((4, tokens, depth), bf16), shaped((tokens, 1), f32), shaped((tokens, 1), f32)],
+        (place, hidden[0]),
+        flops=10 * tokens * width,
+        moved=4 * tokens * width,
+    )
+    own_late, far = lax.optimization_barrier((own, far))
+    mid = lax.ppermute(own_late, "fsdp", mid_route)
+    outer = lax.ppermute(far, "fsdp", outward_route)
+    acc = run(
+        partial_kernel, [vmem] * 4, shaped((padded, tokens), f32), (own, near, far, normed), flops=3 * dot_flops
+    )
+    lg, cross_part = run(
+        lambda *refs: head_kernel(vocab, *refs),
+        [smem] + [vmem] * 5,
+        [shaped((padded, tokens), bf16), shard],
+        (place, acc, mid, outer, normed, targets),
+        flops=2 * dot_flops,
+    )
+    got_mid = lax.ppermute(cross_part, "fsdp", mid_route)
+    got_in = lax.ppermute(cross_part, "fsdp", inward_route)
+    own_part, near_part, far_part = run(
+        grads_kernel, [vmem] * 2, [shard] * 3, (lg, normed), flops=3 * dot_flops
+    )
+    far_sum = run(add_kernel, [vmem] * 2, shard, (far_part, got_in))
+    got_far = lax.ppermute(far_sum, "fsdp", far_route)
+    near_part, _ = lax.optimization_barrier((near_part, got_in))
+    got_near = lax.ppermute(near_part, "fsdp", near_route)
+    grad_hidden = run(
+        hidden_grad_kernel,
+        [smem] + [vmem] * 9,
+        shaped((tokens, width), bf16),
+        (place, lg, own, near, far, mid, outer, hidden[0], mean, inv),
+        [pltpu.VMEM((4, tokens, depth), f32)],
+        flops=4 * dot_flops,
+    )
+    tcount = train_step[0].astype(f32)
+    fix = jnp.stack([1.0 - jnp.exp(tcount * math.log(beta_one)), 1.0 - jnp.exp(tcount * math.log(beta_two))])
+    parts = (own_part, got_near, got_far, got_mid)
+    updated, sent = run(
+        step_kernel,
+        [smem] + [vmem] * 4 + [anywhere] * 3,
+        [shaped((vocab, depth), f32), shard],
+        (fix, *parts, params_t, moment_t, second_t),
+        [dma((3,)), state, state, state],
+    )
+
+    def pair_with_bit(bit_index):
+        def finish(updated, sent, parts, moment_t, second_t):
+            partner = from_partner(sent, "replica", bit_index)
+            moment_new, second_new = run_out(
+                moments_kernel,
+                [vmem] * 4 + [anywhere] * 2,
+                [state_out] * 2,
+                (*parts, moment_t, second_t),
+                [dma((2,)), state, state],
+            )
+            averaged = run_out(
+                average_kernel, [vmem] * 2, [state_out], (updated, partner), [dma, state]
+            )[0]
+            return averaged, moment_new, second_new
+
+        return finish
+
+    levels = lax.axis_size("replica").bit_length() - 1
+    outs = lax.switch(
+        train_step[0] % levels,
+        [pair_with_bit(bit_index) for bit_index in range(levels)],
+        updated, sent, parts, moment_t, second_t,
+    )
+    averaged, moment_new, second_new = (jnp.transpose(out, (1, 2, 0)) for out in outs)
+    return (averaged, moment_new, second_new, grad_hidden[None])
+
+
+def run_out(kernel, ins, outs, args, scratch):
+    return pl.pallas_call(
+        kernel,
+        in_specs=ins,
+        out_specs=[anywhere] * len(outs),
+        out_shape=outs,
+        scratch_shapes=list(scratch),
+        compiler_params=pltpu.CompilerParams(vmem_limit_bytes=24 << 20),
+        cost_estimate=pl.CostEstimate(flops=0, bytes_accessed=6 << 20, transcendentals=0),
+    )(*args)
+
+
+def local(hidden, targets, params, moment, second, train_step):
+    four = lax.axis_size("fsdp") == 4 and params.shape[1] % 128 == 0 and hidden.shape[1] % 128 == 0
+    chosen = local_line if four else local_any
+    return chosen(hidden, targets, params, moment, second, train_step)
+
+
 def solution(mesh):
     placed = (
         P("replica", ("groups", "fsdp"), None),

time: 183 us -> 114 us (0.62)
  waiting for transfers between devices: 133 us -> 61.4 us
  Pallas kernels: 0 us -> 23.6 us
  starting transfers between devices: 0.15 us -> 17.2 us
  between operations: 14.9 us -> 1.58 us
  matrix products: 11.1 us -> 0 us
  other arithmetic: 10.5 us -> 0.08 us
  local copies, waits for them, and re-layouts: 13 us -> 8.86 us
    all_gather x1 -> x0, waiting for transfers between devices: 87.8 us -> none  [local(): weight_bf = lax.all_gather(shard_bf, 'fsdp', axis=0, tiled=True)]
    ppermute x0 -> x8, waiting for transfers between devices: none -> 57.9 us  [the longest x1 23.8 us: local_line(): far = lax.ppermute(own, 'fsdp', far_route)]
    unnamed x3 -> x0, waiting for transfers between devices: 43 us -> none
    pallas_call x0 -> x10, Pallas kernels: none -> 23.6 us  [the longest x8 17.9 us: run(): pl.pallas_call(kernel, in_specs=ins, out_specs=out_specs, out_shape=outs,...]
    ppermute x0 -> x8, starting transfers between devices: none -> 15.6 us  [the longest x1 4.1 us: local_line(): far = lax.ppermute(own, 'fsdp', far_route)]
    dot_general x3 -> x0, matrix products: 11.1 us -> none  [the longest x1 4.26 us: local(): lax.dot_general(logit_grad, weight_bf, (((1,), (1,)), ((), ())), preferre...]
    unnamed x13 -> x38, local copies, waits for them, and re-layouts: 13 us -> 8.86 us
    sub x1 -> x0, other arithmetic: 3.65 us -> none  [local(): updated = params - learn_rate * (adam_step + weight_decay * params)]
  transfers between devices with their start and end apart: 3 -> 9, of which waited for: 3 -> 6; matrix products, arithmetic and copies ran while one was open for 4% -> 0% of each run, Pallas kernels for 0% -> 12%
where the time goes in v1:
time: 114 us; the launch traced here: 113 us
  waiting for transfers between devices  61.4 us (54%)
  Pallas kernels  23.6 us (21%)
  starting transfers between devices  17.2 us (15%)
  local copies, waits for them, and re-layouts  8.86 us (8%)
  between operations  1.58 us (1%)
    ppermute x1, waiting for transfers between devices, local_line(): far = lax.ppermute(own, 'fsdp', far_route)  23.8 us
    pallas_call x8, Pallas kernels, run(): pl.pallas_call(kernel, in_specs=ins, out_specs=out_specs, out_shape=outs,...  17.9 us
    ppermute x1, waiting for transfers between devices, local_line(): got_near = lax.ppermute(near_part, 'fsdp', near_route)  11.2 us
    ppermute x1, waiting for transfers between devices, local_line(): outer = lax.ppermute(far, 'fsdp', outward_route)  10.6 us
    unnamed x38, local copies, waits for them, and re-layouts  8.86 us
    ppermute x1, waiting for transfers between devices, local_line(): got_in = lax.ppermute(cross_part, 'fsdp', inward_route)  8.65 us
    pallas_call x2, Pallas kernels, run_out(): pl.pallas_call(kernel, in_specs=ins, out_specs=[anywhere] * len(outs), ou...  5.69 us
    ppermute x1, starting transfers between devices, local_line(): far = lax.ppermute(own, 'fsdp', far_route)  4.1 us
  transfers between devices with their start and end apart: 9, of which 6 were waited for; matrix products, arithmetic and copies ran while one was open for 0% of the time, Pallas kernels for 12%

profile of v1, /device:TPU:0, one launch (start us, length us, event | category | flops | bytes accessed | tf_op | source)
XLA Modules:
  0.0 113.0 jit_solution(14406015462917774698)
XLA Ops:
  0.6 0.0 copy-start.2
  0.6 1.2 %copy-done.2 = f32[1,640,441]{1,0,2:T(1,128)S(1)} copy-done((f32[1,640,441]{1,0,2:T(1,128)S(1)}, f32[1,640,441]{1,0,2:T(1,128)}, u32[]{:S(2)}) %copy-start.2) | copy-done | bytes 1128984
  1.9 0.8 shard_map.93.own_ref
  2.7 4.1 %collective-permute-start.3 = (bf16[448,640]{1,0:T(8,128)(2,1)S(1)}, bf16[448,640]{1,0:T(8,128)(2,1)S(1)}, u32[]{:S(2)}, u32[]{:S(2)}) collective-permute-start(bf16[448,640]{1,0:T(8,128)(2,1)S(1)} %shard_map.93.own_ref), channel_id=1, source_target_pairs={{0,8},{8,0},{4,12},{12,4},{1,9},{9,1},{5,13},{13,5},{2,10},{10,2},... | collective-permute-start | bytes 1720328 | tf_op jit(solution)/shard_map/ppermute | solution.py:297
  6.8 1.6 %collective-permute-start.2 = (bf16[448,640]{1,0:T(8,128)(2,1)S(1)}, bf16[448,640]{1,0:T(8,128)(2,1)S(1)}, u32[]{:S(2)}, u32[]{:S(2)}) collective-permute-start(bf16[448,640]{1,0:T(8,128)(2,1)S(1)} %shard_map.93.own_ref), channel_id=1, source_target_pairs={{0,4},{4,0},{8,12},{12,8},{1,5},{5,1},{9,13},{13,9},{2,6},{6,2},{1... | collective-permute-start | bytes 1720328 | tf_op jit(solution)/shard_map/ppermute | solution.py:298
  8.4 23.8 %collective-permute-done.3.far_ref = bf16[448,640]{1,0:T(8,128)(2,1)S(1)} collective-permute-done((bf16[448,640]{1,0:T(8,128)(2,1)S(1)}, bf16[448,640]{1,0:T(8,128)(2,1)S(1)}, u32[]{:S(2)}, u32[]{:S(2)}) %collective-permute-start.3) | collective-permute-done | bytes 573472 | tf_op jit(solution)/shard_map/ppermute | solution.py:297
  32.2 0.7 collective-permute-start.4
  32.9 1.3 %collective-permute-start.5 = (bf16[448,640]{1,0:T(8,128)(2,1)S(1)}, bf16[448,640]{1,0:T(8,128)(2,1)S(1)}, u32[]{:S(2)}, u32[]{:S(2)}) collective-permute-start(bf16[448,640]{1,0:T(8,128)(2,1)S(1)} %collective-permute-done.3.far_ref), channel_id=1, source_target_pairs={{4,0},{8,12},{5,1},{9,13},{6,2},{10,14},{7,3},{11,15},{20,16},{24,... | collective-permute-start | bytes 1720328 | tf_op jit(solution)/shard_map/ppermute | solution.py:309
  34.2 0.0 copy-start
  34.2 1.5 %copy-done = bf16[1,384,2560]{2,1,0:T(8,128)(2,1)S(1)} copy-done((bf16[1,384,2560]{2,1,0:T(8,128)(2,1)S(1)}, bf16[1,384,2560]{2,1,0:T(8,128)(2,1)}, u32[]{:S(2)}) %copy-start) | copy-done | bytes 1966104
  35.7 1.6 %shard_map.94 = (bf16[4,384,640]{2,1,0:T(8,128)(2,1)S(1)}, f32[384,1]{1,0:T(8,128)S(1)}, f32[384,1]{1,0:T(8,128)S(1)}) custom-call(s32[1]{0:T(128)} %bitcast.3.place_ref.refs_0_, bf16[384,2560]{1,0:T(8,128)(2,1)S(1)} %bitcast.16), custom_call_target="tpu_custom_call" | custom-call | flops 9830400 | bytes 3932160 | tf_op jit(solution)/shard_map/pallas_call | solution.py:117
  37.3 0.0 copy-start.10
  37.3 0.0 copy-start.12
  37.3 0.0 collective-permute-done.2.near_ref
  37.3 0.0 copy-start.4
  37.4 0.0 copy-start.14
  37.4 1.2 %shard_map.95.refs_1_ = f32[448,384]{1,0:T(8,128)S(1)} custom-call(bf16[448,640]{1,0:T(8,128)(2,1)S(1)} %shard_map.93.own_ref, bf16[448,640]{1,0:T(8,128)(2,1)S(1)} %collective-permute-done.2.near_ref, bf16[448,640]{1,0:T(8,128)(2,1)S(1)} %collective-permute-done.3.far_ref, bf16[4,384,640]{2,1,0:T(8,128)(2,1)S(1)} %get-tuple-element.73.normed_ref.refs_4_), custom_call_target="tpu_custom_call" | custom-call | flops 660602880 | tf_op jit(solution)/shard_map/pallas_call | solution.py:117
  38.5 0.0 copy-done.10
  38.6 0.0 copy-done.12
  38.6 0.0 copy-done.4
  38.6 0.0 collective-permute-done.4.refs_2_.mid_ref
  38.6 0.0 copy-start.6
  38.6 10.6 %collective-permute-done.5.refs_3_.outer_ref = bf16[448,640]{1,0:T(8,128)(2,1)S(1)} collective-permute-done((bf16[448,640]{1,0:T(8,128)(2,1)S(1)}, bf16[448,640]{1,0:T(8,128)(2,1)S(1)}, u32[]{:S(2)}, u32[]{:S(2)}) %collective-permute-start.5) | collective-permute-done | bytes 573472 | tf_op jit(solution)/shard_map/ppermute | solution.py:309
  49.2 0.0 copy-done.14
  49.2 0.0 copy-start.8
  49.2 2.0 %shard_map.96 = (bf16[448,384]{1,0:T(8,128)(2,1)S(1)}, bf16[448,640]{1,0:T(8,128)(2,1)}) custom-call(s32[1]{0:T(128)} %bitcast.3.place_ref.refs_0_, f32[448,384]{1,0:T(8,128)S(1)} %shard_map.95.refs_1_, bf16[448,640]{1,0:T(8,128)(2,1)S(1)} %collective-permute-done.4.refs_2_.mid_ref, bf16[448,640]{1,0:T(8,128)(2,1)S(1)} %collective-permute-done.5.refs_3_.outer_ref, ...), custom_call_target="tpu_custom_call" | custom-call | flops 440401920 | tf_op jit(solution)/shard_map/pallas_call | solution.py:117
  51.2 0.0 copy-done.6
  51.2 0.0 copy-done.8
  51.2 2.4 %collective-permute-start.6 = (bf16[448,640]{1,0:T(8,128)(2,1)}, bf16[448,640]{1,0:T(8,128)(2,1)S(1)}, u32[]{:S(2)}, u32[]{:S(2)}) collective-permute-start(bf16[448,640]{1,0:T(8,128)(2,1)} %get-tuple-element.78), channel_id=1, source_target_pairs={{0,4},{12,8},{1,5},{13,9},{2,6},{14,10},{3,7},{15,11},{16,20},{28,... | collective-permute-start | bytes 1720328 | tf_op jit(solution)/shard_map/ppermute | solution.py:321
  53.6 1.5 %collective-permute-start.9 = (bf16[448,640]{1,0:T(8,128)(2,1)}, bf16[448,640]{1,0:T(8,128)(2,1)}, u32[]{:S(2)}, u32[]{:S(2)}) collective-permute-start(bf16[448,640]{1,0:T(8,128)(2,1)} %get-tuple-element.78), channel_id=1, source_target_pairs={{4,8},{8,4},{5,9},{9,5},{6,10},{10,6},{7,11},{11,7},{20,24},{24,20... | collective-permute-start | bytes 1720328 | tf_op jit(solution)/shard_map/ppermute | solution.py:320
  55.1 0.0 copy-start.1
  55.1 1.7 %shard_map.97 = (bf16[448,640]{1,0:T(8,128)(2,1)}, bf16[448,640]{1,0:T(8,128)(2,1)}, bf16[448,640]{1,0:T(8,128)(2,1)S(1)}) custom-call(bf16[448,384]{1,0:T(8,128)(2,1)S(1)} %get-tuple-element.75.lg_ref, bf16[4,384,640]{2,1,0:T(8,128)(2,1)S(1)} %get-tuple-element.73.normed_ref.refs_4_), custom_call_target="tpu_custom_call" | custom-call | flops 660602880 | tf_op jit(solution)/shard_map/pallas_call | solution.py:117
  56.7 8.7 %collective-permute-done.6.b_ref = bf16[448,640]{1,0:T(8,128)(2,1)S(1)} collective-permute-done((bf16[448,640]{1,0:T(8,128)(2,1)}, bf16[448,640]{1,0:T(8,128)(2,1)S(1)}, u32[]{:S(2)}, u32[]{:S(2)}) %collective-permute-start.6) | collective-permute-done | bytes 573472 | tf_op jit(solution)/shard_map/ppermute | solution.py:321
  65.4 2.4 %collective-permute-start.7 = (bf16[448,640]{1,0:T(8,128)(2,1)}, bf16[448,640]{1,0:T(8,128)(2,1)}, u32[]{:S(2)}, u32[]{:S(2)}) collective-permute-start(bf16[448,640]{1,0:T(8,128)(2,1)} %get-tuple-element.79), channel_id=1, source_target_pairs={{0,4},{4,0},{8,12},{12,8},{1,5},{5,1},{9,13},{13,9},{2,6},{6,2},{1... | collective-permute-start | bytes 1720328 | tf_op jit(solution)/shard_map/ppermute | solution.py:328
  67.8 1.0 shard_map.98
  68.7 1.7 %collective-permute-start.8 = (bf16[448,640]{1,0:T(8,128)(2,1)}, bf16[448,640]{1,0:T(8,128)(2,1)}, u32[]{:S(2)}, u32[]{:S(2)}) collective-permute-start(bf16[448,640]{1,0:T(8,128)(2,1)} %shard_map.98), channel_id=1, source_target_pairs={{0,8},{8,0},{4,12},{12,4},{1,9},{9,1},{5,13},{13,5},{2,10},{10,2},... | collective-permute-start | bytes 1720328 | tf_op jit(solution)/shard_map/ppermute | solution.py:326
  71.2 0.1 pad_maximum_fusion.fix_ref
  71.3 0.0 copy-done.1
  71.3 0.0 copy-start.5
  71.3 1.1 copy-done.5
  72.3 0.0 copy-start.7
  72.3 1.1 copy-done.7
  73.4 0.0 copy-start.9
  73.4 1.1 copy-done.9
  74.5 0.0 copy-start.11
  74.5 0.9 copy-done.11
  75.4 0.0 copy-start.13
  75.4 0.9 copy-done.13
  76.3 4.1 %shard_map.100 = bf16[384,2560]{1,0:T(8,128)(2,1)} custom-call(s32[1]{0:T(128)} %bitcast.3.place_ref.refs_0_, bf16[448,384]{1,0:T(8,128)(2,1)S(1)} %get-tuple-element.75.lg_ref, bf16[448,640]{1,0:T(8,128)(2,1)S(1)} %shard_map.93.own_ref, bf16[448,640]{1,0:T(8,128)(2,1)S(1)} %copy-done.5, bf16[448,640]{1,0:T(8,128)(2,1)S(1)} %collective-permute-done.3.far_ref, ...), custom_call_target="tpu_custom_call" | custom-call | flops 880803840 | tf_op jit(solution)/shard_map/pallas_call | solution.py:117
  80.4 0.0 collective-permute-done.9.mid_ref
  80.4 11.2 %collective-permute-done.7.near_ref = bf16[448,640]{1,0:T(8,128)(2,1)} collective-permute-done((bf16[448,640]{1,0:T(8,128)(2,1)}, bf16[448,640]{1,0:T(8,128)(2,1)}, u32[]{:S(2)}, u32[]{:S(2)}) %collective-permute-start.7) | collective-permute-done | bytes 573472 | tf_op jit(solution)/shard_map/ppermute | solution.py:328
  91.6 3.6 %collective-permute-done.8.far_ref = bf16[448,640]{1,0:T(8,128)(2,1)} collective-permute-done((bf16[448,640]{1,0:T(8,128)(2,1)}, bf16[448,640]{1,0:T(8,128)(2,1)}, u32[]{:S(2)}, u32[]{:S(2)}) %collective-permute-start.8) | collective-permute-done | bytes 573472 | tf_op jit(solution)/shard_map/ppermute | solution.py:326
  95.2 0.0 copy-done.3
  95.2 0.0 copy-done.15
  95.2 0.0 copy-done.16
  95.3 0.0 copy-done.17
  95.3 5.7 %shard_map.99 = (f32[441,640]{1,0:T(8,128)S(1)}, bf16[448,640]{1,0:T(8,128)(2,1)S(1)}) custom-call(f32[2]{0:T(128)S(1)} %pad_maximum_fusion.fix_ref, bf16[448,640]{1,0:T(8,128)(2,1)S(1)} %copy-done.17, bf16[448,640]{1,0:T(8,128)(2,1)} %collective-permute-done.7.near_ref, bf16[448,640]{1,0:T(8,128)(2,1)} %collective-permute-done.8.far_ref, ...), custom_call_target="tpu_custom_call" | custom-call | tf_op jit(solution)/shard_map/pallas_call | solution.py:117
  100.9 11.0 %conditional.1 = (f32[441,1,640]{2,1,0:T(1,128)S(1)}, f32[441,1,640]{2,1,0:T(1,128)}, f32[441,1,640]{2,1,0:T(1,128)}) conditional(s32[]{:T(128)} %clamp.3, (bf16[448,640]{1,0:T(8,128)(2,1)S(1)}, f32[441,640]{1,0:T(8,128)S(1)}, bf16[448,640]{1,0:T(8,128)(2,1)S(1)}, bf16[448,640]{1,0:T(8,128)(2,1)}, bf16[448,640]{1,0:T(8,128)(2,1)}, ...), branch_computations={%region_0.1_spmd, %region_1.2_spmd} | conditional | bytes 14876736 | solution.py:366
  101.2 1.6 %collective-permute-start.1 = (bf16[448,640]{1,0:T(8,128)(2,1)S(1)}, bf16[448,640]{1,0:T(8,128)(2,1)S(1)}, u32[]{:S(2)}, u32[]{:S(2)}) collective-permute-start(bf16[448,640]{1,0:T(8,128)(2,1)S(1)} %get-tuple-element.43), channel_id=1, source_target_pairs={{0,2},{2,0},{1,3},{3,1},{4,6},{6,4},{5,7},{7,5},{8,10},{10,8},{9,1... | collective-permute-start | bytes 1720328 | tf_op jit(solution)/shard_map/cond/branch_1_fun/ppermute | solution.py:30
  102.8 4.7 %branch_1_fun.3 = (f32[441,1,640]{2,1,0:T(1,128)}, f32[441,1,640]{2,1,0:T(1,128)}) custom-call(bf16[448,640]{1,0:T(8,128)(2,1)S(1)} %get-tuple-element.44.own_ref, bf16[448,640]{1,0:T(8,128)(2,1)} %get-tuple-element.45.near_ref, bf16[448,640]{1,0:T(8,128)(2,1)} %get-tuple-element.46.far_ref, bf16[448,640]{1,0:T(8,128)(2,1)} %get-tuple-element.47.mid_ref, ...), custom_call_target="tpu_custom_call" | custom-call | bytes 6291456 | tf_op jit(solution)/shard_map/cond/branch_1_fun/pallas_call | solution.py:376
  107.4 3.5 %collective-permute-done.1.partner_ref = bf16[448,640]{1,0:T(8,128)(2,1)S(1)} collective-permute-done((bf16[448,640]{1,0:T(8,128)(2,1)S(1)}, bf16[448,640]{1,0:T(8,128)(2,1)S(1)}, u32[]{:S(2)}, u32[]{:S(2)}) %collective-permute-start.1) | collective-permute-done | bytes 573472 | tf_op jit(solution)/shard_map/cond/branch_1_fun/ppermute | solution.py:30
  111.0 1.0 branch_1_fun.2
  112.0 0.0 copy-start.18
  112.0 1.0 copy-done.18
  (4 shorter events, 0.0 us)
Async XLA Ops:
  0.6 1.3 %copy-start.2 = (f32[1,640,441]{1,0,2:T(1,128)S(1)}, f32[1,640,441]{1,0,2:T(1,128)}, u32[]{:S(2)}) copy-start(f32[1,640,441]{1,0,2:T(1,128)} %param.10) | copy-start | bytes 3386884
  2.7 29.5 %collective-permute-start.3 = (bf16[448,640]{1,0:T(8,128)(2,1)S(1)}, bf16[448,640]{1,0:T(8,128)(2,1)S(1)}, u32[]{:S(2)}, u32[]{:S(2)}) collective-permute-start(bf16[448,640]{1,0:T(8,128)(2,1)S(1)} %shard_map.93.own_ref), channel_id=1, source_target_pairs={{0,8},{8,0},{4,12},{12,4},{1,9},{9,1},{5,13},{13,5},{2,10},{10,2},... | collective-permute-start | bytes 1720328 | tf_op jit(solution)/shard_map/ppermute | solution.py:297
  6.8 30.5 %collective-permute-start.2 = (bf16[448,640]{1,0:T(8,128)(2,1)S(1)}, bf16[448,640]{1,0:T(8,128)(2,1)S(1)}, u32[]{:S(2)}, u32[]{:S(2)}) collective-permute-start(bf16[448,640]{1,0:T(8,128)(2,1)S(1)} %shard_map.93.own_ref), channel_id=1, source_target_pairs={{0,4},{4,0},{8,12},{12,8},{1,5},{5,1},{9,13},{13,9},{2,6},{6,2},{1... | collective-permute-start | bytes 1720328 | tf_op jit(solution)/shard_map/ppermute | solution.py:298
  32.2 6.4 %collective-permute-start.4 = (bf16[448,640]{1,0:T(8,128)(2,1)S(1)}, bf16[448,640]{1,0:T(8,128)(2,1)S(1)}, u32[]{:S(2)}, u32[]{:S(2)}) collective-permute-start(bf16[448,640]{1,0:T(8,128)(2,1)S(1)} %shard_map.93.own_ref), channel_id=1, source_target_pairs={{4,8},{8,4},{5,9},{9,5},{6,10},{10,6},{7,11},{11,7},{20,24},{24,20... | collective-permute-start | bytes 1720328 | tf_op jit(solution)/shard_map/ppermute | solution.py:308
  32.9 16.3 %collective-permute-start.5 = (bf16[448,640]{1,0:T(8,128)(2,1)S(1)}, bf16[448,640]{1,0:T(8,128)(2,1)S(1)}, u32[]{:S(2)}, u32[]{:S(2)}) collective-permute-start(bf16[448,640]{1,0:T(8,128)(2,1)S(1)} %collective-permute-done.3.far_ref), channel_id=1, source_target_pairs={{4,0},{8,12},{5,1},{9,13},{6,2},{10,14},{7,3},{11,15},{20,16},{24,... | collective-permute-start | bytes 1720328 | tf_op jit(solution)/shard_map/ppermute | solution.py:309
  34.2 1.5 %copy-start = (bf16[1,384,2560]{2,1,0:T(8,128)(2,1)S(1)}, bf16[1,384,2560]{2,1,0:T(8,128)(2,1)}, u32[]{:S(2)}) copy-start(bf16[1,384,2560]{2,1,0:T(8,128)(2,1)} %param.8) | copy-start | bytes 5898244
  37.3 1.2 %copy-start.10 = (f32[384,1]{1,0:T(8,128)}, f32[384,1]{1,0:T(8,128)S(1)}, u32[]{:S(2)}) copy-start(f32[384,1]{1,0:T(8,128)S(1)} %get-tuple-element.86.mean_ref) | copy-start | bytes 4612
  37.3 1.2 %copy-start.12 = (f32[384,1]{1,0:T(8,128)}, f32[384,1]{1,0:T(8,128)S(1)}, u32[]{:S(2)}) copy-start(f32[384,1]{1,0:T(8,128)S(1)} %get-tuple-element.87.inv_ref) | copy-start | bytes 4612
  37.3 1.2 %copy-start.4 = (bf16[448,640]{1,0:T(8,128)(2,1)}, bf16[448,640]{1,0:T(8,128)(2,1)S(1)}, u32[]{:S(2)}) copy-start(bf16[448,640]{1,0:T(8,128)(2,1)S(1)} %collective-permute-done.2.near_ref) | copy-start | bytes 1720324
  37.4 11.8 %copy-start.14 = (s32[1,384]{1,0:T(1,128)S(1)}, s32[1,384]{1,0:T(1,128)}, u32[]{:S(2)}) copy-start(s32[1,384]{1,0:T(1,128)} %refs_5_.1) | copy-start | bytes 4612
  38.6 12.6 %copy-start.6 = (bf16[448,640]{1,0:T(8,128)(2,1)}, bf16[448,640]{1,0:T(8,128)(2,1)S(1)}, u32[]{:S(2)}) copy-start(bf16[448,640]{1,0:T(8,128)(2,1)S(1)} %collective-permute-done.4.refs_2_.mid_ref) | copy-start | bytes 1720324
  49.2 2.0 %copy-start.8 = (bf16[448,640]{1,0:T(8,128)(2,1)}, bf16[448,640]{1,0:T(8,128)(2,1)S(1)}, u32[]{:S(2)}) copy-start(bf16[448,640]{1,0:T(8,128)(2,1)S(1)} %collective-permute-done.5.refs_3_.outer_ref) | copy-start | bytes 1720324
  51.2 14.2 %collective-permute-start.6 = (bf16[448,640]{1,0:T(8,128)(2,1)}, bf16[448,640]{1,0:T(8,128)(2,1)S(1)}, u32[]{:S(2)}, u32[]{:S(2)}) collective-permute-start(bf16[448,640]{1,0:T(8,128)(2,1)} %get-tuple-element.78), channel_id=1, source_target_pairs={{0,4},{12,8},{1,5},{13,9},{2,6},{14,10},{3,7},{15,11},{16,20},{28,... | collective-permute-start | bytes 1720328 | tf_op jit(solution)/shard_map/ppermute | solution.py:321
  53.6 26.8 %collective-permute-start.9 = (bf16[448,640]{1,0:T(8,128)(2,1)}, bf16[448,640]{1,0:T(8,128)(2,1)}, u32[]{:S(2)}, u32[]{:S(2)}) collective-permute-start(bf16[448,640]{1,0:T(8,128)(2,1)} %get-tuple-element.78), channel_id=1, source_target_pairs={{4,8},{8,4},{5,9},{9,5},{6,10},{10,6},{7,11},{11,7},{20,24},{24,20... | collective-permute-start | bytes 1720328 | tf_op jit(solution)/shard_map/ppermute | solution.py:320
  55.1 16.2 %copy-start.1 = (bf16[1,384,2560]{2,1,0:T(8,128)(2,1)S(1)}, bf16[1,384,2560]{2,1,0:T(8,128)(2,1)}, u32[]{:S(2)}) copy-start(bf16[1,384,2560]{2,1,0:T(8,128)(2,1)} %param.8) | copy-start | bytes 5898244
  65.4 26.2 %collective-permute-start.7 = (bf16[448,640]{1,0:T(8,128)(2,1)}, bf16[448,640]{1,0:T(8,128)(2,1)}, u32[]{:S(2)}, u32[]{:S(2)}) collective-permute-start(bf16[448,640]{1,0:T(8,128)(2,1)} %get-tuple-element.79), channel_id=1, source_target_pairs={{0,4},{4,0},{8,12},{12,8},{1,5},{5,1},{9,13},{13,9},{2,6},{6,2},{1... | collective-permute-start | bytes 1720328 | tf_op jit(solution)/shard_map/ppermute | solution.py:328
  68.7 26.5 %collective-permute-start.8 = (bf16[448,640]{1,0:T(8,128)(2,1)}, bf16[448,640]{1,0:T(8,128)(2,1)}, u32[]{:S(2)}, u32[]{:S(2)}) collective-permute-start(bf16[448,640]{1,0:T(8,128)(2,1)} %shard_map.98), channel_id=1, source_target_pairs={{0,8},{8,0},{4,12},{12,4},{1,9},{9,1},{5,13},{13,5},{2,10},{10,2},... | collective-permute-start | bytes 1720328 | tf_op jit(solution)/shard_map/ppermute | solution.py:326
  71.3 1.1 copy-start.5
  72.3 1.1 copy-start.7
  73.4 1.1 copy-start.9
  74.5 0.9 copy-start.11
  75.4 0.9 copy-start.13
  76.3 18.9 %copy-start.3 = (f32[1,640,441]{1,0,2:T(1,128)S(1)}, f32[1,640,441]{1,0,2:T(1,128)}, u32[]{:S(2)}) copy-start(f32[1,640,441]{1,0,2:T(1,128)} %param.10) | copy-start | bytes 3386884
  76.3 18.9 %copy-start.15 = (f32[1,640,441]{1,0,2:T(1,128)S(1)}, f32[1,640,441]{1,0,2:T(1,128)}, u32[]{:S(2)}) copy-start(f32[1,640,441]{1,0,2:T(1,128)} %param.11) | copy-start | bytes 3386884
  76.3 18.9 %copy-start.16 = (f32[1,640,441]{1,0,2:T(1,128)S(1)}, f32[1,640,441]{1,0,2:T(1,128)}, u32[]{:S(2)}) copy-start(f32[1,640,441]{1,0,2:T(1,128)} %param.12) | copy-start | bytes 3386884
  76.3 18.9 %copy-start.17 = (bf16[448,640]{1,0:T(8,128)(2,1)S(1)}, bf16[448,640]{1,0:T(8,128)(2,1)}, u32[]{:S(2)}) copy-start(bf16[448,640]{1,0:T(8,128)(2,1)} %get-tuple-element.76.own_ref) | copy-start | bytes 1720324
  101.2 9.8 %collective-permute-start.1 = (bf16[448,640]{1,0:T(8,128)(2,1)S(1)}, bf16[448,640]{1,0:T(8,128)(2,1)S(1)}, u32[]{:S(2)}, u32[]{:S(2)}) collective-permute-start(bf16[448,640]{1,0:T(8,128)(2,1)S(1)} %get-tuple-element.43), channel_id=1, source_target_pairs={{0,2},{2,0},{1,3},{3,1},{4,6},{6,4},{5,7},{7,5},{8,10},{10,8},{9,1... | collective-permute-start | bytes 1720328 | tf_op jit(solution)/shard_map/cond/branch_1_fun/ppermute | solution.py:30
  112.0 1.0 copy-start.18

commit v2 on v0

--- a/solution.py
+++ b/solution.py
@@ -3,6 +3,8 @@
 import jax
 import jax.numpy as jnp
 from jax import lax
+from jax.experimental import pallas as pl
+from jax.experimental.pallas import tpu as pltpu
 from jax.sharding import PartitionSpec as P
 
 norm_eps = 1e-05
@@ -47,7 +49,7 @@
     return swap_values
 
 
-def local(hidden, targets, params, moment, second, train_step):
+def local_any(hidden, targets, params, moment, second, train_step):
     normalized, inv_scale = normalize(hidden[0])
     normed_bf = normalized.astype(jnp.bfloat16)
     labels = targets[0]
@@ -92,6 +94,318 @@
     return (averaged, moment_new, second_new, grad_hidden[None])
 
 
+near_route = [(0, 1), (1, 0), (2, 3), (3, 2)]
+far_route = [(0, 2), (2, 0), (1, 3), (3, 1)]
+chunk_rows = 256
+
+f32 = jnp.float32
+bf16 = jnp.bfloat16
+vmem = pl.BlockSpec(memory_space=pltpu.VMEM)
+smem = pl.BlockSpec(memory_space=pltpu.SMEM)
+anywhere = pl.BlockSpec(memory_space=pl.ANY)
+dma = pltpu.SemaphoreType.DMA
+
+
+def shaped(shape, dtype):
+    return jax.ShapeDtypeStruct(shape, dtype)
+
+
+def run(kernel, ins, outs, args, scratch=(), limit=10, flops=0, moved=0, out_specs=None, alias=None):
+    if out_specs is None:
+        out_specs = [vmem] * len(outs)
+    results = pl.pallas_call(
+        kernel,
+        in_specs=ins,
+        out_specs=out_specs,
+        out_shape=outs,
+        scratch_shapes=list(scratch),
+        input_output_aliases=alias or {},
+        compiler_params=pltpu.CompilerParams(vmem_limit_bytes=limit << 20),
+        cost_estimate=pl.CostEstimate(flops=flops, bytes_accessed=moved, transcendentals=0),
+    )(*args)
+    return list(results)
+
+
+def columns(block, width):
+    return pl.ds(pl.multiple_of(block * width, 128), width)
+
+
+def nt_dot(a, b):
+    return lax.dot_general(a, b, (((1,), (1,)), ((), ())), preferred_element_type=f32)
+
+
+def tn_dot(a, b):
+    return lax.dot_general(a, b, (((0,), (0,)), ((), ())), preferred_element_type=f32)
+
+
+def nn_dot(a, b):
+    return jnp.dot(a, b, preferred_element_type=f32)
+
+
+def round_weight_kernel(params_ref, a_ref, b_ref, whole_ref, held_a, held_b, sems):
+    rows = held_a.shape[0]
+    rest = held_b.shape[0]
+    first = pltpu.make_async_copy(params_ref.at[pl.ds(0, rows), 0, :], held_a, sems.at[0])
+    later = pltpu.make_async_copy(params_ref.at[pl.ds(rows, rest), 0, :], held_b, sems.at[1])
+    first.start()
+    later.start()
+    first.wait()
+    rounded = held_a[...].astype(bf16)
+    a_ref[...] = rounded
+    whole_ref[0:rows, :] = rounded
+    later.wait()
+    b_ref[0:rest, :] = held_b[...].astype(bf16)
+    b_ref[rest:, :] = jnp.zeros((b_ref.shape[0] - rest, b_ref.shape[1]), bf16)
+    whole_ref[rows:, :] = b_ref[...]
+
+
+def norm_kernel(hidden_ref, normed_ref, mean_ref, inv_ref):
+    rows, width = hidden_ref.shape
+    depth = normed_ref.shape[2]
+    place = lax.axis_index("fsdp")
+    step = 128
+    for top in range(0, rows, step):
+        part = pl.ds(top, step)
+        values = hidden_ref[part, :].astype(f32)
+        mean = jnp.mean(values, axis=-1, keepdims=True)
+        center = values - mean
+        inv = lax.rsqrt(jnp.mean(center * center, axis=-1, keepdims=True) + norm_eps)
+        mean_ref[part, :] = mean
+        inv_ref[part, :] = inv
+        for slot in range(normed_ref.shape[0]):
+            block = place ^ slot
+            own = hidden_ref[part, columns(block, depth)].astype(f32)
+            normed_ref[slot, part, :] = ((own - mean) * inv).astype(bf16)
+
+
+def tiled_kernel(params_ref, moment_ref, second_ref, params_out, moment_out, second_out, sems):
+    copies = []
+    for slot, (src, dst) in enumerate(
+        ((params_ref, params_out), (moment_ref, moment_out), (second_ref, second_out))
+    ):
+        copies.append(pltpu.make_async_copy(src.at[:, 0, :], dst, sems.at[slot]))
+        copies[-1].start()
+    for copy in copies:
+        copy.wait()
+
+
+def logits_kernel(own_ref, near_ref, far_a, cross_a, far_b, normed_ref, raw_a_ref, acc_b_ref):
+    rows = far_a.shape[0]
+    raw = nt_dot(own_ref[0:rows, :], normed_ref[0]) + nt_dot(near_ref[0:rows, :], normed_ref[1])
+    raw_a_ref[...] = raw + nt_dot(far_a[...], normed_ref[2]) + nt_dot(cross_a[...], normed_ref[3])
+    acc = nt_dot(own_ref[rows:, :], normed_ref[0]) + nt_dot(near_ref[rows:, :], normed_ref[1])
+    acc_b_ref[...] = acc + nt_dot(far_b[...], normed_ref[2])
+
+
+def head_kernel(vocab, raw_a_ref, acc_b_ref, cross_b, normed_ref, labels_ref, lg_a_ref, lg_b_ref, cross_a_ref, cross_b_ref):
+    rows = raw_a_ref.shape[0]
+    raws = (raw_a_ref[...], acc_b_ref[...] + nt_dot(cross_b[...], normed_ref[3]))
+    capped, exps, hots = [], [], []
+    for raw, top in zip(raws, (0, rows)):
+        capped.append(jnp.tanh(raw / logit_cap))
+        ids = lax.broadcasted_iota(jnp.int32, raw.shape, 0) + top
+        exp_logits = jnp.exp(logit_cap * capped[-1])
+        exps.append(jnp.where(ids < vocab, exp_logits, 0.0) if top else exp_logits)
+        hots.append((ids == labels_ref[...]).astype(f32))
+    total = sum(jnp.sum(part, axis=0, keepdims=True) for part in exps)
+    for cap, part, hot, lg_ref, out_ref in zip(
+        capped, exps, hots, (lg_a_ref, lg_b_ref), (cross_a_ref, cross_b_ref)
+    ):
+        logit_grad = ((part / total - hot) * (1.0 - cap * cap)).astype(bf16)
+        lg_ref[...] = logit_grad
+        out_ref[...] = nn_dot(logit_grad, normed_ref[3]).astype(bf16)
+
+
+def grads_kernel(lg_a, lg_b, normed_ref, own_a, own_b, near_a, near_b, far_a, far_b):
+    for slot, outs in ((2, (far_a, far_b)), (1, (near_a, near_b)), (0, (own_a, own_b))):
+        for lg, out in zip((lg_a, lg_b), outs):
+            out[...] = nn_dot(lg[...], normed_ref[slot]).astype(bf16)
+
+
+def add_kernel(a_ref, b_ref, out_ref):
+    out_ref[...] = (a_ref[...].astype(f32) + b_ref[...].astype(f32)).astype(bf16)
+
+
+def hidden_grad_kernel(lg_a, lg_b, *refs):
+    whole, weights_a, weights_b = refs[0:2], refs[2:4], refs[4:6]
+    hidden_ref, mean_ref, inv_ref, out_ref, held = refs[6:]
+    top = lg_a.shape[0]
+    rows, width = hidden_ref.shape
+    slots, _, depth = held.shape
+    place = lax.axis_index("fsdp")
+    mean, inv = mean_ref[...], inv_ref[...]
+    first = jnp.zeros((rows, 1), f32)
+    second = jnp.zeros((rows, 1), f32)
+    for slot in range(slots):
+        if slot < 2:
+            block_a, block_b = whole[slot][0:top, :], whole[slot][top:, :]
+        else:
+            block_a, block_b = weights_a[slot - 2][...], weights_b[slot - 2][...]
+        back = tn_dot(lg_a[...], block_a) + tn_dot(lg_b[...], block_b)
+        held[slot] = back
+        normalized = (hidden_ref[:, columns(place ^ slot, depth)].astype(f32) - mean) * inv
+        first = first + jnp.sum(back, axis=-1, keepdims=True)
+        second = second + jnp.sum(back * normalized, axis=-1, keepdims=True)
+    first, second = first / width, second / width
+    for slot in range(slots):
+        part = columns(place ^ slot, depth)
+        normalized = (hidden_ref[:, part].astype(f32) - mean) * inv
+        out_ref[:, part] = (inv * (held[slot] - first - normalized * second)).astype(bf16)
+
+
+def step_kernel(top, count_ref, own_ref, near_ref, far_ref, params_ref, moment_ref, second_ref, *refs):
+    if top:
+        refs = refs[2:]
+    updated_ref, sent_ref, moment_out, second_out, held_moment, held_second, sems = refs
+    rows = updated_ref.shape[0]
+    part = pl.ds(top, rows)
+    target = pl.ds(0, rows)
+    grads = sum(ref[target, :].astype(f32) for ref in (own_ref, near_ref, far_ref))
+    moment_new = beta_one * moment_ref[part, :] + (1.0 - beta_one) * grads
+    held_moment[...] = moment_new
+    first = pltpu.make_async_copy(held_moment, moment_out.at[part, 0, :], sems.at[0])
+    first.start()
+    second_new = beta_two * second_ref[part, :] + (1.0 - beta_two) * grads * grads
+    held_second[...] = second_new
+    later = pltpu.make_async_copy(held_second, second_out.at[part, 0, :], sems.at[1])
+    later.start()
+    tcount = jnp.full((1, updated_ref.shape[1]), count_ref[0].astype(f32))
+    fix_one = 1.0 / (1.0 - jnp.exp(tcount * math.log(beta_one)))
+    fix_two = 1.0 / (1.0 - jnp.exp(tcount * math.log(beta_two)))
+    adam_step = moment_new * fix_one / (jnp.sqrt(second_new * fix_two) + adam_eps)
+    params = params_ref[part, :]
+    updated = params - learn_rate * (adam_step + weight_decay * params)
+    updated_ref[...] = updated
+    sent_ref[target, :] = updated.astype(bf16)
+    rest = sent_ref.shape[0] - rows
+    if rest:
+        sent_ref[rows:, :] = jnp.zeros((rest, sent_ref.shape[1]), bf16)
+    first.wait()
+    later.wait()
+
+
+def average_kernel(top, levels, count_ref, updated_ref, *refs):
+    partners = refs[:levels]
+    out_ref, held, sem = refs[-3:]
+    rows = held.shape[0]
+    level = lax.rem(count_ref[0], levels)
+    partner = partners[0][0:rows, :]
+    for bit in range(1, levels):
+        partner = jnp.where(level == bit, partners[bit][0:rows, :], partner)
+    held[...] = 0.5 * (updated_ref[...] + partner.astype(f32))
+    copy = pltpu.make_async_copy(held, out_ref.at[pl.ds(top, rows), 0, :], sem)
+    copy.start()
+    copy.wait()
+
+
+def by_vocab(shard):
+    return jnp.transpose(shard, (2, 0, 1))
+
+
+def local_line(hidden, targets, params, moment, second, train_step):
+    tokens, width = hidden.shape[1:]
+    depth, vocab = params.shape[1:]
+    padded = -(-vocab // 16) * 16
+    state_t = [by_vocab(shard) for shard in (params, moment, second)]
+    heights = (chunk_rows, padded - chunk_rows)
+    tops = (0, chunk_rows)
+    counts = (chunk_rows, vocab - chunk_rows)
+    shards = [shaped((height, depth), bf16) for height in heights]
+    held = [pltpu.VMEM((count, depth), f32) for count in counts]
+    state = shaped((vocab, depth), f32)
+    state_out = shaped((vocab, 1, depth), f32)
+    dot_flops = 2 * padded * tokens * depth
+
+    def hop(block, route):
+        return lax.ppermute(block, "fsdp", route)
+
+    whole_shard = shaped((padded, depth), bf16)
+    *own, own_whole = run(
+        round_weight_kernel, [anywhere], [*shards, whole_shard], (state_t[0],), [*held, dma((2,))]
+    )
+    far = [hop(block, far_route) for block in own]
+    near = hop(own_whole, near_route)
+    normed, mean, inv = run(
+        norm_kernel,
+        [vmem],
+        [shaped((4, tokens, depth), bf16), shaped((tokens, 1), f32), shaped((tokens, 1), f32)],
+        (hidden[0],),
+        flops=10 * tokens * width,
+        moved=4 * tokens * width,
+    )
+    tiled = run(tiled_kernel, [anywhere] * 3, [state] * 3, state_t, [dma((3,))])
+    far[0], normed, *tiled = lax.optimization_barrier((far[0], normed, *tiled))
+    cross = [hop(block, near_route) for block in far]
+    raw_a, acc_b = run(
+        logits_kernel,
+        [vmem] * 6,
+        [shaped((height, tokens), f32) for height in heights],
+        (own_whole, near, far[0], cross[0], far[1], normed),
+        flops=3 * dot_flops,
+    )
+    lg_a, lg_b, cross_part_a, cross_part_b = run(
+        lambda *refs: head_kernel(vocab, *refs),
+        [vmem] * 5,
+        [shaped((height, tokens), bf16) for height in heights] + shards,
+        (raw_a, acc_b, cross[1], normed, targets),
+        flops=2 * dot_flops,
+    )
+    got_a, got_b = [hop(block, near_route) for block in (cross_part_a, cross_part_b)]
+    own_a, own_b, near_a, near_b, far_a, far_b = run(
+        grads_kernel, [vmem] * 3, shards * 3, (lg_a, lg_b, normed), flops=3 * dot_flops
+    )
+    sum_a = run(add_kernel, [vmem] * 2, [shards[0]], (far_a, got_a))[0]
+    got_b, near_a, sum_a = lax.optimization_barrier((got_b, near_a, sum_a))
+    sum_b = run(add_kernel, [vmem] * 2, [shards[1]], (far_b, got_b))[0]
+    near_b, sum_b = lax.optimization_barrier((near_b, sum_b))
+    got_far = [hop(block, far_route) for block in (sum_a, sum_b)]
+    got_near = [hop(block, near_route) for block in (near_a, near_b)]
+    grad_hidden = run(
+        hidden_grad_kernel,
+        [vmem] * 11,
+        [shaped((tokens, width), bf16)],
+        (lg_a, lg_b, own_whole, near, far[0], cross[0], far[1], cross[1], hidden[0], mean, inv),
+        [pltpu.VMEM((4, tokens, depth), f32)],
+        flops=4 * dot_flops,
+    )[0]
+    got_far[0], grad_hidden = lax.optimization_barrier((got_far[0], grad_hidden))
+    levels = lax.axis_size("replica").bit_length() - 1
+    updated, partners, moments = [], [], []
+    for index, top in enumerate(tops):
+        fresh, sent, *moments = run(
+            lambda *refs, top=top: step_kernel(top, *refs),
+            [smem] + [vmem] * 6 + [anywhere] * len(moments),
+            [shaped((counts[index], depth), f32), shards[index], state_out, state_out],
+            (train_step, (own_a, own_b)[index], got_near[index], got_far[index], *tiled, *moments),
+            [held[index], held[index], dma((2,))],
+            out_specs=[vmem, vmem, anywhere, anywhere],
+            alias={7: 2, 8: 3} if top else None,
+        )
+        updated.append(fresh)
+        partners.append([from_partner(sent, "replica", bit) for bit in range(levels)])
+    partners[0], updated[1] = lax.optimization_barrier((partners[0], updated[1]))
+    averaged = []
+    for index, top in enumerate(tops):
+        averaged = run(
+            lambda *refs, top=top: average_kernel(top, levels, *refs),
+            [smem] + [vmem] * (1 + levels) + [anywhere] * len(averaged),
+            [state_out],
+            (train_step, updated[index], *partners[index], *averaged),
+            [held[index], dma],
+            out_specs=[anywhere],
+            alias={2 + levels: 0} if top else None,
+        )
+    outs = [jnp.transpose(out, (1, 2, 0)) for out in (averaged[0], *moments)]
+    return (*outs, grad_hidden[None])
+
+
+def local(hidden, targets, params, moment, second, train_step):
+    four = lax.axis_size("fsdp") == 4 and params.shape[1] % 128 == 0 and hidden.shape[1] % 128 == 0
+    four = four and params.shape[2] > chunk_rows
+    chosen = local_line if four else local_any
+    return chosen(hidden, targets, params, moment, second, train_step)
+
+
 def solution(mesh):
     placed = (
         P("replica", ("groups", "fsdp"), None),

time: 183 us -> 97.2 us (0.53)
  waiting for transfers between devices: 133 us -> 57.9 us
  starting transfers between devices: 0.15 us -> 18.5 us
  Pallas kernels: 0 us -> 16.7 us
  between operations: 14.9 us -> 1.39 us
  matrix products: 11.1 us -> 0 us
  other arithmetic: 10.5 us -> 0 us
  local copies, waits for them, and re-layouts: 13 us -> 2.51 us
    all_gather x1 -> x0, waiting for transfers between devices: 87.8 us -> none  [local(): weight_bf = lax.all_gather(shard_bf, 'fsdp', axis=0, tiled=True)]
    ppermute x0 -> x11, waiting for transfers between devices: none -> 50.7 us  [hop(): return lax.ppermute(block, 'fsdp', route)]
    unnamed x3 -> x0, waiting for transfers between devices: 43 us -> none
    pallas_call x0 -> x13, Pallas kernels: none -> 16.7 us  [run(): pl.pallas_call(kernel, in_specs=ins, out_specs=out_specs, out_shape=outs,...]
    ppermute x0 -> x11, starting transfers between devices: none -> 15.4 us  [hop(): return lax.ppermute(block, 'fsdp', route)]
    dot_general x3 -> x0, matrix products: 11.1 us -> none  [the longest x1 4.26 us: local(): lax.dot_general(logit_grad, weight_bf, (((1,), (1,)), ((), ())), preferre...]
    unnamed x13 -> x10, local copies, waits for them, and re-layouts: 13 us -> 2.51 us
    ppermute x1 -> x4, waiting for transfers between devices: 1.97 us -> 7.22 us  [from_partner(): return lax.ppermute(block, axis, route)]
  transfers between devices with their start and end apart: 3 -> 15, of which waited for: 3 -> 10; matrix products, arithmetic and copies ran while one was open for 4% -> 0% of each run, Pallas kernels for 0% -> 14%
where the time goes in v2:
time: 97.2 us; the launch traced here: 97 us
  waiting for transfers between devices  57.9 us (60%)
  starting transfers between devices  18.5 us (19%)
  Pallas kernels  16.7 us (17%)
  local copies, waits for them, and re-layouts  2.51 us (3%)
  between operations  1.39 us (1%)
    ppermute x11, waiting for transfers between devices, hop(): return lax.ppermute(block, 'fsdp', route)  50.7 us
    pallas_call x13, Pallas kernels, run(): pl.pallas_call(kernel, in_specs=ins, out_specs=out_specs, out_shape=outs,...  16.7 us
    ppermute x11, starting transfers between devices, hop(): return lax.ppermute(block, 'fsdp', route)  15.4 us
    ppermute x4, waiting for transfers between devices, from_partner(): return lax.ppermute(block, axis, route)  7.22 us
    ppermute x4, starting transfers between devices, from_partner(): return lax.ppermute(block, axis, route)  3.03 us
    unnamed x10, local copies, waits for them, and re-layouts  2.51 us
  transfers between devices with their start and end apart: 15, of which 10 were waited for; matrix products, arithmetic and copies ran while one was open for 0% of the time, Pallas kernels for 14%

profile of v2, /device:TPU:0, one launch (start us, length us, event | category | flops | bytes accessed | tf_op | source)
XLA Modules:
  0.0 97.0 jit_solution(18433404243225329978)
XLA Ops:
  0.6 0.0 copy-start.1
  0.6 1.2 %copy-done.1 = f32[1,640,441]{1,0,2:T(1,128)S(1)} copy-done((f32[1,640,441]{1,0,2:T(1,128)S(1)}, f32[1,640,441]{1,0,2:T(1,128)}, u32[]{:S(2)}) %copy-start.1) | copy-done | bytes 1128984
  1.9 0.0 copy-start.2
  1.9 0.9 shard_map.93
  2.8 4.1 %collective-permute-start.1 = (bf16[256,640]{1,0:T(8,128)(2,1)S(1)}, bf16[256,640]{1,0:T(8,128)(2,1)S(1)}, u32[]{:S(2)}, u32[]{:S(2)}) collective-permute-start(bf16[256,640]{1,0:T(8,128)(2,1)S(1)} %get-tuple-element.49), channel_id=1, source_target_pairs={{0,8},{8,0},{4,12},{12,4},{1,9},{9,1},{5,13},{13,5},{2,10},{10,2},... | collective-permute-start | bytes 983048 | tf_op jit(solution)/shard_map/ppermute | solution.py:320
  6.9 1.6 %collective-permute-start = (bf16[448,640]{1,0:T(8,128)(2,1)S(1)}, bf16[448,640]{1,0:T(8,128)(2,1)S(1)}, u32[]{:S(2)}, u32[]{:S(2)}) collective-permute-start(bf16[448,640]{1,0:T(8,128)(2,1)S(1)} %get-tuple-element.48.own_ref.refs_0_), channel_id=1, source_target_pairs={{0,4},{4,0},{8,12},{12,8},{1,5},{5,1},{9,13},{13,9},{2,6},{6,2},{1... | collective-permute-start | bytes 1720328 | tf_op jit(solution)/shard_map/ppermute | solution.py:320
  8.5 0.3 collective-permute-start.3
  8.8 0.0 copy-done.2
  8.8 0.0 copy-start.3
  8.8 1.3 %copy-done.3 = f32[1,640,441]{1,0,2:T(1,128)S(1)} copy-done((f32[1,640,441]{1,0,2:T(1,128)S(1)}, f32[1,640,441]{1,0,2:T(1,128)}, u32[]{:S(2)}) %copy-start.3) | copy-done | bytes 1128984
  10.0 0.0 copy-start
  10.0 2.3 %shard_map.95 = (f32[441,640]{1,0:T(8,128)S(1)}, f32[441,640]{1,0:T(8,128)S(1)}, f32[441,640]{1,0:T(8,128)S(1)}) custom-call(f32[441,1,640]{2,1,0:T(1,128)S(1)} %bitcast.11, f32[441,1,640]{2,1,0:T(1,128)S(1)} %bitcast.12, f32[441,1,640]{2,1,0:T(1,128)S(1)} %bitcast.13), custom_call_target="tpu_custom_call" | custom-call | tf_op jit(solution)/shard_map/pallas_call | solution.py:116
  12.4 0.0 copy-done
  12.4 1.6 %shard_map.94 = (bf16[4,384,640]{2,1,0:T(8,128)(2,1)S(1)}, f32[384,1]{1,0:T(8,128)S(1)}, f32[384,1]{1,0:T(8,128)S(1)}) custom-call(bf16[384,2560]{1,0:T(8,128)(2,1)S(1)} %bitcast.8), custom_call_target="tpu_custom_call" | custom-call | flops 9830400 | bytes 3932160 | tf_op jit(solution)/shard_map/pallas_call | solution.py:116
  14.0 8.6 %collective-permute-done.1.far_a.refs_2_ = bf16[256,640]{1,0:T(8,128)(2,1)S(1)} collective-permute-done((bf16[256,640]{1,0:T(8,128)(2,1)S(1)}, bf16[256,640]{1,0:T(8,128)(2,1)S(1)}, u32[]{:S(2)}, u32[]{:S(2)}) %collective-permute-start.1) | collective-permute-done | bytes 327712 | tf_op jit(solution)/shard_map/ppermute | solution.py:320
  22.5 0.0 copy-start.4
  22.5 0.0 collective-permute-start.2
  22.5 10.0 %collective-permute-done.3.far_b.refs_4_ = bf16[192,640]{1,0:T(8,128)(2,1)S(1)} collective-permute-done((bf16[192,640]{1,0:T(8,128)(2,1)S(1)}, bf16[192,640]{1,0:T(8,128)(2,1)S(1)}, u32[]{:S(2)}, u32[]{:S(2)}) %collective-permute-start.3) | collective-permute-done | bytes 245792 | tf_op jit(solution)/shard_map/ppermute | solution.py:320
  32.6 2.3 %collective-permute-start.4 = (bf16[192,640]{1,0:T(8,128)(2,1)S(1)}, bf16[192,640]{1,0:T(8,128)(2,1)S(1)}, u32[]{:S(2)}, u32[]{:S(2)}) collective-permute-start(bf16[192,640]{1,0:T(8,128)(2,1)S(1)} %collective-permute-done.3.far_b.refs_4_), channel_id=1, source_target_pairs={{0,4},{4,0},{8,12},{12,8},{1,5},{5,1},{9,13},{13,9},{2,6},{6,2},{1... | collective-permute-start | bytes 737288 | tf_op jit(solution)/shard_map/ppermute | solution.py:320
  34.9 0.0 collective-permute-done.near_ref.refs_1_
  34.9 6.0 %collective-permute-done.2.cross_a.refs_3_ = bf16[256,640]{1,0:T(8,128)(2,1)S(1)} collective-permute-done((bf16[256,640]{1,0:T(8,128)(2,1)S(1)}, bf16[256,640]{1,0:T(8,128)(2,1)S(1)}, u32[]{:S(2)}, u32[]{:S(2)}) %collective-permute-start.2) | collective-permute-done | bytes 327712 | tf_op jit(solution)/shard_map/ppermute | solution.py:320
  40.9 1.4 %shard_map.96 = (f32[256,384]{1,0:T(8,128)S(1)}, f32[192,384]{1,0:T(8,128)S(1)}) custom-call(bf16[448,640]{1,0:T(8,128)(2,1)S(1)} %get-tuple-element.48.own_ref.refs_0_, bf16[448,640]{1,0:T(8,128)(2,1)S(1)} %collective-permute-done.near_ref.refs_1_, bf16[256,640]{1,0:T(8,128)(2,1)S(1)} %collective-permute-done.1.far_a.refs_2_, ...), custom_call_target="tpu_custom_call" | custom-call | flops 660602880 | tf_op jit(solution)/shard_map/pallas_call | solution.py:116
  42.3 2.4 %collective-permute-done.4.refs_2_.refs_5_ = bf16[192,640]{1,0:T(8,128)(2,1)S(1)} collective-permute-done((bf16[192,640]{1,0:T(8,128)(2,1)S(1)}, bf16[192,640]{1,0:T(8,128)(2,1)S(1)}, u32[]{:S(2)}, u32[]{:S(2)}) %collective-permute-start.4) | collective-permute-done | bytes 245792 | tf_op jit(solution)/shard_map/ppermute | solution.py:320
  44.7 0.0 copy-done.4
  44.7 1.1 %shard_map.97 = (bf16[256,384]{1,0:T(8,128)(2,1)S(1)}, bf16[192,384]{1,0:T(8,128)(2,1)S(1)}, bf16[256,640]{1,0:T(8,128)(2,1)S(1)}, bf16[192,640]{1,0:T(8,128)(2,1)S(1)}) custom-call(f32[256,384]{1,0:T(8,128)S(1)} %get-tuple-element.57.refs_0_, f32[192,384]{1,0:T(8,128)S(1)} %get-tuple-element.58.refs_1_, ...), custom_call_target="tpu_custom_call" | custom-call | flops 440401920 | tf_op jit(solution)/shard_map/pallas_call | solution.py:116
  45.8 1.5 %collective-permute-start.6 = (bf16[256,640]{1,0:T(8,128)(2,1)S(1)}, bf16[256,640]{1,0:T(8,128)(2,1)S(1)}, u32[]{:S(2)}, u32[]{:S(2)}) collective-permute-start(bf16[256,640]{1,0:T(8,128)(2,1)S(1)} %get-tuple-element.65), channel_id=1, source_target_pairs={{0,4},{4,0},{8,12},{12,8},{1,5},{5,1},{9,13},{13,9},{2,6},{6,2},{1... | collective-permute-start | bytes 983048 | tf_op jit(solution)/shard_map/ppermute | solution.py:320
  47.3 0.5 collective-permute-start.5
  47.9 1.1 %shard_map.98 = (bf16[256,640]{1,0:T(8,128)(2,1)S(1)}, bf16[192,640]{1,0:T(8,128)(2,1)S(1)}, bf16[256,640]{1,0:T(8,128)(2,1)S(1)}, bf16[192,640]{1,0:T(8,128)(2,...) custom-call(bf16[256,384]{1,0:T(8,128)(2,1)S(1)} %get-tuple-element.59.lg_a, ...), custom_call_target="tpu_custom_call" | custom-call | flops 660602880 | tf_op jit(solution)/shard_map/pallas_call | solution.py:116
  49.0 7.5 %collective-permute-done.6.b_ref = bf16[256,640]{1,0:T(8,128)(2,1)S(1)} collective-permute-done((bf16[256,640]{1,0:T(8,128)(2,1)S(1)}, bf16[256,640]{1,0:T(8,128)(2,1)S(1)}, u32[]{:S(2)}, u32[]{:S(2)}) %collective-permute-start.6) | collective-permute-done | bytes 327712 | tf_op jit(solution)/shard_map/ppermute | solution.py:320
  56.5 0.1 shard_map.99
  56.6 2.9 %collective-permute-done.5.b_ref = bf16[192,640]{1,0:T(8,128)(2,1)S(1)} collective-permute-done((bf16[192,640]{1,0:T(8,128)(2,1)S(1)}, bf16[192,640]{1,0:T(8,128)(2,1)S(1)}, u32[]{:S(2)}, u32[]{:S(2)}) %collective-permute-start.5) | collective-permute-done | bytes 245792 | tf_op jit(solution)/shard_map/ppermute | solution.py:320
  59.4 1.7 %collective-permute-start.8 = (bf16[256,640]{1,0:T(8,128)(2,1)S(1)}, bf16[256,640]{1,0:T(8,128)(2,1)S(1)}, u32[]{:S(2)}, u32[]{:S(2)}) collective-permute-start(bf16[256,640]{1,0:T(8,128)(2,1)S(1)} %shard_map.99), channel_id=1, source_target_pairs={{0,8},{8,0},{4,12},{12,4},{1,9},{9,1},{5,13},{13,5},{2,10},{10,2},... | collective-permute-start | bytes 983048 | tf_op jit(solution)/shard_map/ppermute | solution.py:320
  61.1 1.4 %collective-permute-start.7 = (bf16[256,640]{1,0:T(8,128)(2,1)S(1)}, bf16[256,640]{1,0:T(8,128)(2,1)S(1)}, u32[]{:S(2)}, u32[]{:S(2)}) collective-permute-start(bf16[256,640]{1,0:T(8,128)(2,1)S(1)} %get-tuple-element.66), channel_id=1, source_target_pairs={{0,4},{4,0},{8,12},{12,8},{1,5},{5,1},{9,13},{13,9},{2,6},{6,2},{1... | collective-permute-start | bytes 983048 | tf_op jit(solution)/shard_map/ppermute | solution.py:320
  62.6 0.1 shard_map.102
  62.6 0.6 collective-permute-start.11
  63.3 1.3 %collective-permute-start.12 = (bf16[192,640]{1,0:T(8,128)(2,1)S(1)}, bf16[192,640]{1,0:T(8,128)(2,1)S(1)}, u32[]{:S(2)}, u32[]{:S(2)}) collective-permute-start(bf16[192,640]{1,0:T(8,128)(2,1)S(1)} %shard_map.102), channel_id=1, source_target_pairs={{0,8},{8,0},{4,12},{12,4},{1,9},{9,1},{5,13},{13,5},{2,10},{10,2},... | collective-permute-start | bytes 737288 | tf_op jit(solution)/shard_map/ppermute | solution.py:320
  65.2 4.0 %shard_map.100 = bf16[384,2560]{1,0:T(8,128)(2,1)} custom-call(bf16[256,384]{1,0:T(8,128)(2,1)S(1)} %get-tuple-element.59.lg_a, bf16[192,384]{1,0:T(8,128)(2,1)S(1)} %get-tuple-element.60.lg_b, bf16[448,640]{1,0:T(8,128)(2,1)S(1)} %get-tuple-element.48.own_ref.refs_0_, bf16[448,640]{1,0:T(8,128)(2,1)S(1)} %collective-permute-done.near_ref.refs_1_, ...), custom_call_target="tpu_custom_call" | custom-call | flops 880803840 | tf_op jit(solution)/shard_map/pallas_call | solution.py:116
  69.2 7.3 %collective-permute-done.8.refs_3_ = bf16[256,640]{1,0:T(8,128)(2,1)S(1)} collective-permute-done((bf16[256,640]{1,0:T(8,128)(2,1)S(1)}, bf16[256,640]{1,0:T(8,128)(2,1)S(1)}, u32[]{:S(2)}, u32[]{:S(2)}) %collective-permute-start.8) | collective-permute-done | bytes 327712 | tf_op jit(solution)/shard_map/ppermute | solution.py:320
  76.5 6.1 %collective-permute-done.7.refs_2_ = bf16[256,640]{1,0:T(8,128)(2,1)S(1)} collective-permute-done((bf16[256,640]{1,0:T(8,128)(2,1)S(1)}, bf16[256,640]{1,0:T(8,128)(2,1)S(1)}, u32[]{:S(2)}, u32[]{:S(2)}) %collective-permute-start.7) | collective-permute-done | bytes 327712 | tf_op jit(solution)/shard_map/ppermute | solution.py:320
  82.5 1.2 %shard_map.101 = (f32[256,640]{1,0:T(8,128)S(1)}, bf16[256,640]{1,0:T(8,128)(2,1)S(1)}, f32[441,1,640]{2,1,0:T(1,128)}, f32[441,1,640]{2,1,0:T(1,128)}) custom-call(s32[1]{0:T(128)S(6)} %copy.16.refs_0_, bf16[256,640]{1,0:T(8,128)(2,1)S(1)} %get-tuple-element.61.refs_1_, bf16[256,640]{1,0:T(8,128)(2,1)S(1)} %collective-permute-done.7.refs_2_, ...), custom_call_target="tpu_custom_call" | custom-call | tf_op jit(solution)/shard_map/pallas_call | solution.py:116
  83.8 1.5 %collective-permute-start.10 = (bf16[256,640]{1,0:T(8,128)(2,1)S(1)}, bf16[256,640]{1,0:T(8,128)(2,1)S(1)}, u32[]{:S(2)}, u32[]{:S(2)}) collective-permute-start(bf16[256,640]{1,0:T(8,128)(2,1)S(1)} %get-tuple-element.74), channel_id=1, source_target_pairs={{0,2},{2,0},{1,3},{3,1},{4,6},{6,4},{5,7},{7,5},{8,10},{10,8},{9,1... | collective-permute-start | bytes 983048 | tf_op jit(solution)/shard_map/ppermute | solution.py:30
  85.3 0.0 collective-permute-start.9
  85.3 0.0 collective-permute-done.11.refs_2_
  85.3 0.0 collective-permute-done.12.refs_3_
  85.3 1.2 %shard_map.103 = (f32[185,640]{1,0:T(8,128)S(1)}, bf16[192,640]{1,0:T(8,128)(2,1)S(1)}, f32[441,1,640]{2,1,0:T(1,128)}, f32[441,1,640]{2,1,0:T(1,128)}) custom-call(s32[1]{0:T(128)S(6)} %copy.16.refs_0_, bf16[192,640]{1,0:T(8,128)(2,1)S(1)} %get-tuple-element.75.refs_1_, ...), custom_call_target="tpu_custom_call", output_to_operand_aliasing={{2}: (7, {}), {3}: (8, {})} | custom-call | tf_op jit(solution)/shard_map/pallas_call | solution.py:116
  86.5 1.5 %collective-permute-start.14 = (bf16[192,640]{1,0:T(8,128)(2,1)S(1)}, bf16[192,640]{1,0:T(8,128)(2,1)S(1)}, u32[]{:S(2)}, u32[]{:S(2)}) collective-permute-start(bf16[192,640]{1,0:T(8,128)(2,1)S(1)} %get-tuple-element.85), channel_id=1, source_target_pairs={{0,2},{2,0},{1,3},{3,1},{4,6},{6,4},{5,7},{7,5},{8,10},{10,8},{9,1... | collective-permute-start | bytes 737288 | tf_op jit(solution)/shard_map/ppermute | solution.py:30
  88.0 0.0 collective-permute-start.13
  88.0 4.1 %collective-permute-done.10.refs_3_ = bf16[256,640]{1,0:T(8,128)(2,1)S(1)} collective-permute-done((bf16[256,640]{1,0:T(8,128)(2,1)S(1)}, bf16[256,640]{1,0:T(8,128)(2,1)S(1)}, u32[]{:S(2)}, u32[]{:S(2)}) %collective-permute-start.10) | collective-permute-done | bytes 327712 | tf_op jit(solution)/shard_map/ppermute | solution.py:30
  92.1 0.0 collective-permute-done.9.refs_2_
  92.1 0.9 shard_map.104.refs_4_
  93.0 3.2 %collective-permute-done.14.refs_3_ = bf16[192,640]{1,0:T(8,128)(2,1)S(1)} collective-permute-done((bf16[192,640]{1,0:T(8,128)(2,1)S(1)}, bf16[192,640]{1,0:T(8,128)(2,1)S(1)}, u32[]{:S(2)}, u32[]{:S(2)}) %collective-permute-start.14) | collective-permute-done | bytes 245792 | tf_op jit(solution)/shard_map/ppermute | solution.py:30
  96.2 0.0 collective-permute-done.13.refs_2_
  96.2 0.8 shard_map.105
Async XLA Ops:
  0.6 1.3 %copy-start.1 = (f32[1,640,441]{1,0,2:T(1,128)S(1)}, f32[1,640,441]{1,0,2:T(1,128)}, u32[]{:S(2)}) copy-start(f32[1,640,441]{1,0,2:T(1,128)} %param.8) | copy-start | bytes 3386884
  1.9 6.9 %copy-start.2 = (f32[1,640,441]{1,0,2:T(1,128)S(1)}, f32[1,640,441]{1,0,2:T(1,128)}, u32[]{:S(2)}) copy-start(f32[1,640,441]{1,0,2:T(1,128)} %param.9) | copy-start | bytes 3386884
  2.8 19.8 %collective-permute-start.1 = (bf16[256,640]{1,0:T(8,128)(2,1)S(1)}, bf16[256,640]{1,0:T(8,128)(2,1)S(1)}, u32[]{:S(2)}, u32[]{:S(2)}) collective-permute-start(bf16[256,640]{1,0:T(8,128)(2,1)S(1)} %get-tuple-element.49), channel_id=1, source_target_pairs={{0,8},{8,0},{4,12},{12,4},{1,9},{9,1},{5,13},{13,5},{2,10},{10,2},... | collective-permute-start | bytes 983048 | tf_op jit(solution)/shard_map/ppermute | solution.py:320
  6.9 28.0 %collective-permute-start = (bf16[448,640]{1,0:T(8,128)(2,1)S(1)}, bf16[448,640]{1,0:T(8,128)(2,1)S(1)}, u32[]{:S(2)}, u32[]{:S(2)}) collective-permute-start(bf16[448,640]{1,0:T(8,128)(2,1)S(1)} %get-tuple-element.48.own_ref.refs_0_), channel_id=1, source_target_pairs={{0,4},{4,0},{8,12},{12,8},{1,5},{5,1},{9,13},{13,9},{2,6},{6,2},{1... | collective-permute-start | bytes 1720328 | tf_op jit(solution)/shard_map/ppermute | solution.py:320
  8.5 24.1 %collective-permute-start.3 = (bf16[192,640]{1,0:T(8,128)(2,1)S(1)}, bf16[192,640]{1,0:T(8,128)(2,1)S(1)}, u32[]{:S(2)}, u32[]{:S(2)}) collective-permute-start(bf16[192,640]{1,0:T(8,128)(2,1)S(1)} %get-tuple-element.55), channel_id=1, source_target_pairs={{0,8},{8,0},{4,12},{12,4},{1,9},{9,1},{5,13},{13,5},{2,10},{10,2},... | collective-permute-start | bytes 737288 | tf_op jit(solution)/shard_map/ppermute | solution.py:320
  8.8 1.3 %copy-start.3 = (f32[1,640,441]{1,0,2:T(1,128)S(1)}, f32[1,640,441]{1,0,2:T(1,128)}, u32[]{:S(2)}) copy-start(f32[1,640,441]{1,0,2:T(1,128)} %param.10) | copy-start | bytes 3386884
  10.0 2.3 %copy-start = (bf16[1,384,2560]{2,1,0:T(8,128)(2,1)S(1)}, bf16[1,384,2560]{2,1,0:T(8,128)(2,1)}, u32[]{:S(2)}) copy-start(bf16[1,384,2560]{2,1,0:T(8,128)(2,1)} %param.6) | copy-start | bytes 5898244
  22.5 22.2 %copy-start.4 = (s32[1,384]{1,0:T(1,128)S(1)}, s32[1,384]{1,0:T(1,128)}, u32[]{:S(2)}) copy-start(s32[1,384]{1,0:T(1,128)} %refs_4_.1) | copy-start | bytes 4612
  22.5 18.4 %collective-permute-start.2 = (bf16[256,640]{1,0:T(8,128)(2,1)S(1)}, bf16[256,640]{1,0:T(8,128)(2,1)S(1)}, u32[]{:S(2)}, u32[]{:S(2)}) collective-permute-start(bf16[256,640]{1,0:T(8,128)(2,1)S(1)} %collective-permute-done.1.far_a.refs_2_), channel_id=1, source_target_pairs={{0,4},{4,0},{8,12},{12,8},{1,5},{5,1},{9,13},{13,9},{2,6},{6,2},{1... | collective-permute-start | bytes 983048 | tf_op jit(solution)/shard_map/ppermute | solution.py:320
  32.6 12.1 %collective-permute-start.4 = (bf16[192,640]{1,0:T(8,128)(2,1)S(1)}, bf16[192,640]{1,0:T(8,128)(2,1)S(1)}, u32[]{:S(2)}, u32[]{:S(2)}) collective-permute-start(bf16[192,640]{1,0:T(8,128)(2,1)S(1)} %collective-permute-done.3.far_b.refs_4_), channel_id=1, source_target_pairs={{0,4},{4,0},{8,12},{12,8},{1,5},{5,1},{9,13},{13,9},{2,6},{6,2},{1... | collective-permute-start | bytes 737288 | tf_op jit(solution)/shard_map/ppermute | solution.py:320
  45.8 10.7 %collective-permute-start.6 = (bf16[256,640]{1,0:T(8,128)(2,1)S(1)}, bf16[256,640]{1,0:T(8,128)(2,1)S(1)}, u32[]{:S(2)}, u32[]{:S(2)}) collective-permute-start(bf16[256,640]{1,0:T(8,128)(2,1)S(1)} %get-tuple-element.65), channel_id=1, source_target_pairs={{0,4},{4,0},{8,12},{12,8},{1,5},{5,1},{9,13},{13,9},{2,6},{6,2},{1... | collective-permute-start | bytes 983048 | tf_op jit(solution)/shard_map/ppermute | solution.py:320
  47.3 12.1 %collective-permute-start.5 = (bf16[192,640]{1,0:T(8,128)(2,1)S(1)}, bf16[192,640]{1,0:T(8,128)(2,1)S(1)}, u32[]{:S(2)}, u32[]{:S(2)}) collective-permute-start(bf16[192,640]{1,0:T(8,128)(2,1)S(1)} %get-tuple-element.62), channel_id=1, source_target_pairs={{0,4},{4,0},{8,12},{12,8},{1,5},{5,1},{9,13},{13,9},{2,6},{6,2},{1... | collective-permute-start | bytes 737288 | tf_op jit(solution)/shard_map/ppermute | solution.py:320
  59.4 17.0 %collective-permute-start.8 = (bf16[256,640]{1,0:T(8,128)(2,1)S(1)}, bf16[256,640]{1,0:T(8,128)(2,1)S(1)}, u32[]{:S(2)}, u32[]{:S(2)}) collective-permute-start(bf16[256,640]{1,0:T(8,128)(2,1)S(1)} %shard_map.99), channel_id=1, source_target_pairs={{0,8},{8,0},{4,12},{12,4},{1,9},{9,1},{5,13},{13,5},{2,10},{10,2},... | collective-permute-start | bytes 983048 | tf_op jit(solution)/shard_map/ppermute | solution.py:320
  61.1 21.4 %collective-permute-start.7 = (bf16[256,640]{1,0:T(8,128)(2,1)S(1)}, bf16[256,640]{1,0:T(8,128)(2,1)S(1)}, u32[]{:S(2)}, u32[]{:S(2)}) collective-permute-start(bf16[256,640]{1,0:T(8,128)(2,1)S(1)} %get-tuple-element.66), channel_id=1, source_target_pairs={{0,4},{4,0},{8,12},{12,8},{1,5},{5,1},{9,13},{13,9},{2,6},{6,2},{1... | collective-permute-start | bytes 983048 | tf_op jit(solution)/shard_map/ppermute | solution.py:320
  62.6 22.7 %collective-permute-start.11 = (bf16[192,640]{1,0:T(8,128)(2,1)S(1)}, bf16[192,640]{1,0:T(8,128)(2,1)S(1)}, u32[]{:S(2)}, u32[]{:S(2)}) collective-permute-start(bf16[192,640]{1,0:T(8,128)(2,1)S(1)} %get-tuple-element.79), channel_id=1, source_target_pairs={{0,4},{4,0},{8,12},{12,8},{1,5},{5,1},{9,13},{13,9},{2,6},{6,2},{1... | collective-permute-start | bytes 737288 | tf_op jit(solution)/shard_map/ppermute | solution.py:320
  63.3 22.0 %collective-permute-start.12 = (bf16[192,640]{1,0:T(8,128)(2,1)S(1)}, bf16[192,640]{1,0:T(8,128)(2,1)S(1)}, u32[]{:S(2)}, u32[]{:S(2)}) collective-permute-start(bf16[192,640]{1,0:T(8,128)(2,1)S(1)} %shard_map.102), channel_id=1, source_target_pairs={{0,8},{8,0},{4,12},{12,4},{1,9},{9,1},{5,13},{13,5},{2,10},{10,2},... | collective-permute-start | bytes 737288 | tf_op jit(solution)/shard_map/ppermute | solution.py:320
  83.8 8.3 %collective-permute-start.10 = (bf16[256,640]{1,0:T(8,128)(2,1)S(1)}, bf16[256,640]{1,0:T(8,128)(2,1)S(1)}, u32[]{:S(2)}, u32[]{:S(2)}) collective-permute-start(bf16[256,640]{1,0:T(8,128)(2,1)S(1)} %get-tuple-element.74), channel_id=1, source_target_pairs={{0,2},{2,0},{1,3},{3,1},{4,6},{6,4},{5,7},{7,5},{8,10},{10,8},{9,1... | collective-permute-start | bytes 983048 | tf_op jit(solution)/shard_map/ppermute | solution.py:30
  85.3 6.8 %collective-permute-start.9 = (bf16[256,640]{1,0:T(8,128)(2,1)S(1)}, bf16[256,640]{1,0:T(8,128)(2,1)S(1)}, u32[]{:S(2)}, u32[]{:S(2)}) collective-permute-start(bf16[256,640]{1,0:T(8,128)(2,1)S(1)} %get-tuple-element.74), channel_id=1, source_target_pairs={{0,1},{1,0},{2,3},{3,2},{4,5},{5,4},{6,7},{7,6},{8,9},{9,8},{10,11... | collective-permute-start | bytes 983048 | tf_op jit(solution)/shard_map/ppermute | solution.py:30
  86.5 9.7 %collective-permute-start.14 = (bf16[192,640]{1,0:T(8,128)(2,1)S(1)}, bf16[192,640]{1,0:T(8,128)(2,1)S(1)}, u32[]{:S(2)}, u32[]{:S(2)}) collective-permute-start(bf16[192,640]{1,0:T(8,128)(2,1)S(1)} %get-tuple-element.85), channel_id=1, source_target_pairs={{0,2},{2,0},{1,3},{3,1},{4,6},{6,4},{5,7},{7,5},{8,10},{10,8},{9,1... | collective-permute-start | bytes 737288 | tf_op jit(solution)/shard_map/ppermute | solution.py:30
  88.0 8.2 %collective-permute-start.13 = (bf16[192,640]{1,0:T(8,128)(2,1)S(1)}, bf16[192,640]{1,0:T(8,128)(2,1)S(1)}, u32[]{:S(2)}, u32[]{:S(2)}) collective-permute-start(bf16[192,640]{1,0:T(8,128)(2,1)S(1)} %get-tuple-element.85), channel_id=1, source_target_pairs={{0,1},{1,0},{2,3},{3,2},{4,5},{5,4},{6,7},{7,6},{8,9},{9,8},{10,11... | collective-permute-start | bytes 737288 | tf_op jit(solution)/shard_map/ppermute | solution.py:30

commit v3 on v2

--- a/solution.py
+++ b/solution.py
@@ -103,6 +103,7 @@
 vmem = pl.BlockSpec(memory_space=pltpu.VMEM)
 smem = pl.BlockSpec(memory_space=pltpu.SMEM)
 anywhere = pl.BlockSpec(memory_space=pl.ANY)
+hbm = pl.BlockSpec(memory_space=pltpu.HBM)
 dma = pltpu.SemaphoreType.DMA
 
 
@@ -142,24 +143,36 @@
     return jnp.dot(a, b, preferred_element_type=f32)
 
 
-def round_weight_kernel(params_ref, a_ref, b_ref, whole_ref, held_a, held_b, sems):
-    rows = held_a.shape[0]
-    rest = held_b.shape[0]
-    first = pltpu.make_async_copy(params_ref.at[pl.ds(0, rows), 0, :], held_a, sems.at[0])
-    later = pltpu.make_async_copy(params_ref.at[pl.ds(rows, rest), 0, :], held_b, sems.at[1])
-    first.start()
-    later.start()
-    first.wait()
-    rounded = held_a[...].astype(bf16)
-    a_ref[...] = rounded
-    whole_ref[0:rows, :] = rounded
-    later.wait()
-    b_ref[0:rest, :] = held_b[...].astype(bf16)
+def fetch(src, top, held, sems):
+    rows = held.shape[0]
+    pieces = sems.shape[0]
+    step = -(-rows // pieces // 8) * 8
+    copies = []
+    for piece in range(pieces):
+        start = piece * step
+        count = min(step, rows - start)
+        copies.append(
+            pltpu.make_async_copy(
+                src.at[pl.ds(top + start, count), 0, :], held.at[pl.ds(start, count)], sems.at[piece]
+            )
+        )
+        copies[-1].start()
+    for copy in copies:
+        copy.wait()
+
+
+def round_weight_kernel(params_ref, a_ref, b_ref, whole_ref, held, sems):
+    rows, total = a_ref.shape[0], held.shape[0]
+    rest = total - rows
+    fetch(params_ref, 0, held, sems)
+    a_ref[...] = held[0:rows, :].astype(bf16)
+    b_ref[0:rest, :] = held[rows:, :].astype(bf16)
     b_ref[rest:, :] = jnp.zeros((b_ref.shape[0] - rest, b_ref.shape[1]), bf16)
+    whole_ref[0:rows, :] = a_ref[...]
     whole_ref[rows:, :] = b_ref[...]
 
 
-def norm_kernel(hidden_ref, normed_ref, mean_ref, inv_ref):
+def norm_kernel(_, hidden_ref, normed_ref, mean_ref, inv_ref):
     rows, width = hidden_ref.shape
     depth = normed_ref.shape[2]
     place = lax.axis_index("fsdp")
@@ -253,22 +266,16 @@
         out_ref[:, part] = (inv * (held[slot] - first - normalized * second)).astype(bf16)
 
 
-def step_kernel(top, count_ref, own_ref, near_ref, far_ref, params_ref, moment_ref, second_ref, *refs):
-    if top:
-        refs = refs[2:]
-    updated_ref, sent_ref, moment_out, second_out, held_moment, held_second, sems = refs
+def step_kernel(top, count_ref, own_ref, near_ref, far_ref, params_ref, moment_ref, second_ref,
+                updated_ref, sent_ref, moment_out, second_out):
     rows = updated_ref.shape[0]
     part = pl.ds(top, rows)
     target = pl.ds(0, rows)
     grads = sum(ref[target, :].astype(f32) for ref in (own_ref, near_ref, far_ref))
     moment_new = beta_one * moment_ref[part, :] + (1.0 - beta_one) * grads
-    held_moment[...] = moment_new
-    first = pltpu.make_async_copy(held_moment, moment_out.at[part, 0, :], sems.at[0])
-    first.start()
     second_new = beta_two * second_ref[part, :] + (1.0 - beta_two) * grads * grads
-    held_second[...] = second_new
-    later = pltpu.make_async_copy(held_second, second_out.at[part, 0, :], sems.at[1])
-    later.start()
+    moment_out[...] = moment_new
+    second_out[...] = second_new
     tcount = jnp.full((1, updated_ref.shape[1]), count_ref[0].astype(f32))
     fix_one = 1.0 / (1.0 - jnp.exp(tcount * math.log(beta_one)))
     fix_two = 1.0 / (1.0 - jnp.exp(tcount * math.log(beta_two)))
@@ -280,8 +287,19 @@
     rest = sent_ref.shape[0] - rows
     if rest:
         sent_ref[rows:, :] = jnp.zeros((rest, sent_ref.shape[1]), bf16)
-    first.wait()
-    later.wait()
+
+
+def store_kernel(top, moment_ref, second_ref, *refs):
+    moment_out, second_out, sems = refs[-3:]
+    part = pl.ds(top, moment_ref.shape[0])
+    copies = [
+        pltpu.make_async_copy(moment_ref, moment_out.at[part, 0, :], sems.at[0]),
+        pltpu.make_async_copy(second_ref, second_out.at[part, 0, :], sems.at[1]),
+    ]
+    for copy in copies:
+        copy.start()
+    for copy in copies:
+        copy.wait()
 
 
 def average_kernel(top, levels, count_ref, updated_ref, *refs):
@@ -321,19 +339,23 @@
 
     whole_shard = shaped((padded, depth), bf16)
     *own, own_whole = run(
-        round_weight_kernel, [anywhere], [*shards, whole_shard], (state_t[0],), [*held, dma((2,))]
+        round_weight_kernel,
+        [hbm],
+        [*shards, whole_shard],
+        (state_t[0],),
+        [pltpu.VMEM((vocab, depth), f32), dma((4,))],
     )
     far = [hop(block, far_route) for block in own]
     near = hop(own_whole, near_route)
     normed, mean, inv = run(
         norm_kernel,
-        [vmem],
+        [smem, vmem],
         [shaped((4, tokens, depth), bf16), shaped((tokens, 1), f32), shaped((tokens, 1), f32)],
-        (hidden[0],),
+        (train_step, hidden[0]),
         flops=10 * tokens * width,
         moved=4 * tokens * width,
     )
-    tiled = run(tiled_kernel, [anywhere] * 3, [state] * 3, state_t, [dma((3,))])
+    tiled = run(tiled_kernel, [hbm] * 3, [state] * 3, state_t, [dma((3,))])
     far[0], normed, *tiled = lax.optimization_barrier((far[0], normed, *tiled))
     cross = [hop(block, near_route) for block in far]
     raw_a, acc_b = run(
@@ -355,34 +377,45 @@
         grads_kernel, [vmem] * 3, shards * 3, (lg_a, lg_b, normed), flops=3 * dot_flops
     )
     sum_a = run(add_kernel, [vmem] * 2, [shards[0]], (far_a, got_a))[0]
-    got_b, near_a, sum_a = lax.optimization_barrier((got_b, near_a, sum_a))
+    near_a, later_a = lax.optimization_barrier((near_a, sum_a))
+    got_far_a, got_near_a = hop(sum_a, far_route), hop(near_a, near_route)
+    got_b, later_a = lax.optimization_barrier((got_b, later_a))
     sum_b = run(add_kernel, [vmem] * 2, [shards[1]], (far_b, got_b))[0]
-    near_b, sum_b = lax.optimization_barrier((near_b, sum_b))
-    got_far = [hop(block, far_route) for block in (sum_a, sum_b)]
-    got_near = [hop(block, near_route) for block in (near_a, near_b)]
+    lg_late, sum_b = lax.optimization_barrier((lg_a, sum_b))
     grad_hidden = run(
         hidden_grad_kernel,
         [vmem] * 11,
         [shaped((tokens, width), bf16)],
-        (lg_a, lg_b, own_whole, near, far[0], cross[0], far[1], cross[1], hidden[0], mean, inv),
+        (lg_late, lg_b, own_whole, near, far[0], cross[0], far[1], cross[1], hidden[0], mean, inv),
         [pltpu.VMEM((4, tokens, depth), f32)],
         flops=4 * dot_flops,
     )[0]
-    got_far[0], grad_hidden = lax.optimization_barrier((got_far[0], grad_hidden))
+    got_far_a, got_near_a, sum_b, near_b, grad_hidden = lax.optimization_barrier(
+        (got_far_a, got_near_a, sum_b, near_b, grad_hidden)
+    )
+    got_far = [got_far_a, hop(sum_b, far_route)]
+    got_near = [got_near_a, hop(near_b, near_route)]
     levels = lax.axis_size("replica").bit_length() - 1
     updated, partners, moments = [], [], []
     for index, top in enumerate(tops):
-        fresh, sent, *moments = run(
+        state_part = shaped((counts[index], depth), f32)
+        fresh, sent, *state_new = run(
             lambda *refs, top=top: step_kernel(top, *refs),
-            [smem] + [vmem] * 6 + [anywhere] * len(moments),
-            [shaped((counts[index], depth), f32), shards[index], state_out, state_out],
-            (train_step, (own_a, own_b)[index], got_near[index], got_far[index], *tiled, *moments),
-            [held[index], held[index], dma((2,))],
-            out_specs=[vmem, vmem, anywhere, anywhere],
-            alias={7: 2, 8: 3} if top else None,
+            [smem] + [vmem] * 6,
+            [state_part, shards[index], state_part, state_part],
+            (train_step, (own_a, own_b)[index], got_near[index], got_far[index], *tiled),
         )
         updated.append(fresh)
         partners.append([from_partner(sent, "replica", bit) for bit in range(levels)])
+        moments = run(
+            lambda *refs, top=top: store_kernel(top, *refs),
+            [vmem] * 2 + [anywhere] * len(moments),
+            [state_out] * 2,
+            (*state_new, *moments),
+            [dma((2,))],
+            out_specs=[anywhere] * 2,
+            alias={2: 0, 3: 1} if top else None,
+        )
     partners[0], updated[1] = lax.optimization_barrier((partners[0], updated[1]))
     averaged = []
     for index, top in enumerate(tops):

time: 97.2 us -> 92.5 us (0.952)
  waiting for transfers between devices: 57.9 us -> 46.2 us
  starting transfers between devices: 18.5 us -> 22.9 us
  local copies, waits for them, and re-layouts: 2.51 us -> 3.76 us
  Pallas kernels: 16.7 us -> 17.8 us
    ppermute x11, waiting for transfers between devices: 50.7 us -> 44.5 us  [hop(): return lax.ppermute(block, 'fsdp', route)]
    ppermute x4, waiting for transfers between devices: 7.22 us -> 1.71 us  [from_partner(): return lax.ppermute(block, axis, route)]
    ppermute x11, starting transfers between devices: 15.4 us -> 19.8 us  [hop(): return lax.ppermute(block, 'fsdp', route)]
    unnamed x10 -> x12, local copies, waits for them, and re-layouts: 2.51 us -> 3.76 us
    pallas_call x13 -> x15, Pallas kernels: 16.7 us -> 17.8 us  [run(): pl.pallas_call(kernel, in_specs=ins, out_specs=out_specs, out_shape=outs,...]
  transfers between devices with their start and end apart: 15 -> 15, of which waited for: 10 -> 11; matrix products, arithmetic and copies ran while one was open for 0% -> 0% of each run, Pallas kernels for 14% -> 16%
where the time goes in v3:
time: 92.5 us; the launch traced here: 92 us
  waiting for transfers between devices  46.2 us (50%)
  starting transfers between devices  22.9 us (25%)
  Pallas kernels  17.8 us (19%)
  local copies, waits for them, and re-layouts  3.76 us (4%)
  between operations  1.43 us (2%)
    ppermute x11, waiting for transfers between devices, hop(): return lax.ppermute(block, 'fsdp', route)  44.5 us
    ppermute x11, starting transfers between devices, hop(): return lax.ppermute(block, 'fsdp', route)  19.8 us
    pallas_call x15, Pallas kernels, run(): pl.pallas_call(kernel, in_specs=ins, out_specs=out_specs, out_shape=outs,...  17.8 us
    unnamed x12, local copies, waits for them, and re-layouts  3.76 us
    ppermute x4, starting transfers between devices, from_partner(): return lax.ppermute(block, axis, route)  3.12 us
  transfers between devices with their start and end apart: 15, of which 11 were waited for; matrix products, arithmetic and copies ran while one was open for 0% of the time, Pallas kernels for 16%

profile of v3, /device:TPU:0, one launch (start us, length us, event | category | flops | bytes accessed | tf_op | source)
XLA Modules:
  0.0 92.0 jit_solution(1528554358965045526)
XLA Ops:
  0.6 0.0 copy-start.1
  0.6 1.2 %copy-done.1 = f32[1,640,441]{1,0,2:T(1,128)S(1)} copy-done((f32[1,640,441]{1,0,2:T(1,128)S(1)}, f32[1,640,441]{1,0,2:T(1,128)}, u32[]{:S(2)}) %copy-start.1) | copy-done | bytes 1128984
  1.9 0.0 copy-start.2
  1.9 0.9 shard_map.93
  2.8 4.1 %collective-permute-start.1 = (bf16[256,640]{1,0:T(8,128)(2,1)S(1)}, bf16[256,640]{1,0:T(8,128)(2,1)S(1)}, u32[]{:S(2)}, u32[]{:S(2)}) collective-permute-start(bf16[256,640]{1,0:T(8,128)(2,1)S(1)} %get-tuple-element.54), channel_id=1, source_target_pairs={{0,8},{8,0},{4,12},{12,4},{1,9},{9,1},{5,13},{13,5},{2,10},{10,2},... | collective-permute-start | bytes 983048 | tf_op jit(solution)/shard_map/ppermute | solution.py:338
  6.9 1.6 %collective-permute-start = (bf16[448,640]{1,0:T(8,128)(2,1)S(1)}, bf16[448,640]{1,0:T(8,128)(2,1)S(1)}, u32[]{:S(2)}, u32[]{:S(2)}) collective-permute-start(bf16[448,640]{1,0:T(8,128)(2,1)S(1)} %get-tuple-element.53.own_ref.refs_0_), channel_id=1, source_target_pairs={{0,4},{4,0},{8,12},{12,8},{1,5},{5,1},{9,13},{13,9},{2,6},{6,2},{1... | collective-permute-start | bytes 1720328 | tf_op jit(solution)/shard_map/ppermute | solution.py:338
  8.5 0.3 collective-permute-start.3
  9.5 0.0 copy-done.2
  9.5 0.0 copy-start.3
  9.5 1.2 %copy-done.3 = f32[1,640,441]{1,0,2:T(1,128)S(1)} copy-done((f32[1,640,441]{1,0,2:T(1,128)S(1)}, f32[1,640,441]{1,0,2:T(1,128)}, u32[]{:S(2)}) %copy-start.3) | copy-done | bytes 1128984
  10.7 0.0 copy-start.4
  10.7 1.3 %copy-done.4 = f32[1,640,441]{1,0,2:T(1,128)S(1)} copy-done((f32[1,640,441]{1,0,2:T(1,128)S(1)}, f32[1,640,441]{1,0,2:T(1,128)}, u32[]{:S(2)}) %copy-start.4) | copy-done | bytes 1128984
  12.0 0.0 copy-start
  12.0 2.3 %shard_map.95 = (f32[441,640]{1,0:T(8,128)S(1)}, f32[441,640]{1,0:T(8,128)S(1)}, f32[441,640]{1,0:T(8,128)S(1)}) custom-call(f32[441,1,640]{2,1,0:T(1,128)S(1)} %bitcast.11, f32[441,1,640]{2,1,0:T(1,128)S(1)} %bitcast.12, f32[441,1,640]{2,1,0:T(1,128)S(1)} %bitcast.13), custom_call_target="tpu_custom_call" | custom-call | tf_op jit(solution)/shard_map/pallas_call | solution.py:117
  14.3 0.0 copy-done
  14.3 1.6 %shard_map.94 = (bf16[4,384,640]{2,1,0:T(8,128)(2,1)S(1)}, f32[384,1]{1,0:T(8,128)S(1)}, f32[384,1]{1,0:T(8,128)S(1)}) custom-call(s32[1]{0:T(128)S(6)} %copy.16._.refs_0_, bf16[384,2560]{1,0:T(8,128)(2,1)S(1)} %bitcast.8), custom_call_target="tpu_custom_call" | custom-call | flops 9830400 | bytes 3932160 | tf_op jit(solution)/shard_map/pallas_call | solution.py:117
  15.9 6.7 %collective-permute-done.1.far_a.refs_2_ = bf16[256,640]{1,0:T(8,128)(2,1)S(1)} collective-permute-done((bf16[256,640]{1,0:T(8,128)(2,1)S(1)}, bf16[256,640]{1,0:T(8,128)(2,1)S(1)}, u32[]{:S(2)}, u32[]{:S(2)}) %collective-permute-start.1) | collective-permute-done | bytes 327712 | tf_op jit(solution)/shard_map/ppermute | solution.py:338
  22.6 0.0 copy-start.5
  22.6 0.0 collective-permute-start.2
  22.6 10.0 %collective-permute-done.3.far_b.refs_4_ = bf16[192,640]{1,0:T(8,128)(2,1)S(1)} collective-permute-done((bf16[192,640]{1,0:T(8,128)(2,1)S(1)}, bf16[192,640]{1,0:T(8,128)(2,1)S(1)}, u32[]{:S(2)}, u32[]{:S(2)}) %collective-permute-start.3) | collective-permute-done | bytes 245792 | tf_op jit(solution)/shard_map/ppermute | solution.py:338
  32.6 2.3 %collective-permute-start.4 = (bf16[192,640]{1,0:T(8,128)(2,1)S(1)}, bf16[192,640]{1,0:T(8,128)(2,1)S(1)}, u32[]{:S(2)}, u32[]{:S(2)}) collective-permute-start(bf16[192,640]{1,0:T(8,128)(2,1)S(1)} %collective-permute-done.3.far_b.refs_4_), channel_id=1, source_target_pairs={{0,4},{4,0},{8,12},{12,8},{1,5},{5,1},{9,13},{13,9},{2,6},{6,2},{1... | collective-permute-start | bytes 737288 | tf_op jit(solution)/shard_map/ppermute | solution.py:338
  34.9 0.0 collective-permute-done.near_ref.refs_1_
  34.9 6.0 %collective-permute-done.2.cross_a.refs_3_ = bf16[256,640]{1,0:T(8,128)(2,1)S(1)} collective-permute-done((bf16[256,640]{1,0:T(8,128)(2,1)S(1)}, bf16[256,640]{1,0:T(8,128)(2,1)S(1)}, u32[]{:S(2)}, u32[]{:S(2)}) %collective-permute-start.2) | collective-permute-done | bytes 327712 | tf_op jit(solution)/shard_map/ppermute | solution.py:338
  40.9 1.4 %shard_map.96 = (f32[256,384]{1,0:T(8,128)S(1)}, f32[192,384]{1,0:T(8,128)S(1)}) custom-call(bf16[448,640]{1,0:T(8,128)(2,1)S(1)} %get-tuple-element.53.own_ref.refs_0_, bf16[448,640]{1,0:T(8,128)(2,1)S(1)} %collective-permute-done.near_ref.refs_1_, bf16[256,640]{1,0:T(8,128)(2,1)S(1)} %collective-permute-done.1.far_a.refs_2_, ...), custom_call_target="tpu_custom_call" | custom-call | flops 660602880 | tf_op jit(solution)/shard_map/pallas_call | solution.py:117
  42.4 2.4 %collective-permute-done.4.refs_2_.refs_5_ = bf16[192,640]{1,0:T(8,128)(2,1)S(1)} collective-permute-done((bf16[192,640]{1,0:T(8,128)(2,1)S(1)}, bf16[192,640]{1,0:T(8,128)(2,1)S(1)}, u32[]{:S(2)}, u32[]{:S(2)}) %collective-permute-start.4) | collective-permute-done | bytes 245792 | tf_op jit(solution)/shard_map/ppermute | solution.py:338
  44.7 0.0 copy-done.5
  44.7 1.1 %shard_map.97 = (bf16[256,384]{1,0:T(8,128)(2,1)S(1)}, bf16[192,384]{1,0:T(8,128)(2,1)S(1)}, bf16[256,640]{1,0:T(8,128)(2,1)S(1)}, bf16[192,640]{1,0:T(8,128)(2,1)S(1)}) custom-call(f32[256,384]{1,0:T(8,128)S(1)} %get-tuple-element.62.refs_0_, f32[192,384]{1,0:T(8,128)S(1)} %get-tuple-element.63.refs_1_, ...), custom_call_target="tpu_custom_call" | custom-call | flops 440401920 | tf_op jit(solution)/shard_map/pallas_call | solution.py:117
  45.8 1.6 %collective-permute-start.5 = (bf16[256,640]{1,0:T(8,128)(2,1)S(1)}, bf16[256,640]{1,0:T(8,128)(2,1)S(1)}, u32[]{:S(2)}, u32[]{:S(2)}) collective-permute-start(bf16[256,640]{1,0:T(8,128)(2,1)S(1)} %get-tuple-element.68), channel_id=1, source_target_pairs={{0,4},{4,0},{8,12},{12,8},{1,5},{5,1},{9,13},{13,9},{2,6},{6,2},{1... | collective-permute-start | bytes 983048 | tf_op jit(solution)/shard_map/ppermute | solution.py:338
  47.4 0.5 collective-permute-start.8
  47.9 1.2 %shard_map.98 = (bf16[256,640]{1,0:T(8,128)(2,1)S(1)}, bf16[192,640]{1,0:T(8,128)(2,1)S(1)}, bf16[256,640]{1,0:T(8,128)(2,1)S(1)}, bf16[192,640]{1,0:T(8,128)(2,...) custom-call(bf16[256,384]{1,0:T(8,128)(2,1)S(1)} %get-tuple-element.75.lg_a, ...), custom_call_target="tpu_custom_call" | custom-call | flops 660602880 | tf_op jit(solution)/shard_map/pallas_call | solution.py:117
  49.1 7.5 %collective-permute-done.5.b_ref = bf16[256,640]{1,0:T(8,128)(2,1)S(1)} collective-permute-done((bf16[256,640]{1,0:T(8,128)(2,1)S(1)}, bf16[256,640]{1,0:T(8,128)(2,1)S(1)}, u32[]{:S(2)}, u32[]{:S(2)}) %collective-permute-start.5) | collective-permute-done | bytes 327712 | tf_op jit(solution)/shard_map/ppermute | solution.py:338
  56.5 0.1 shard_map.99
  56.6 1.6 %collective-permute-start.7 = (bf16[256,640]{1,0:T(8,128)(2,1)S(1)}, bf16[256,640]{1,0:T(8,128)(2,1)S(1)}, u32[]{:S(2)}, u32[]{:S(2)}) collective-permute-start(bf16[256,640]{1,0:T(8,128)(2,1)S(1)} %get-tuple-element.70), channel_id=1, source_target_pairs={{0,4},{4,0},{8,12},{12,8},{1,5},{5,1},{9,13},{13,9},{2,6},{6,2},{1... | collective-permute-start | bytes 983048 | tf_op jit(solution)/shard_map/ppermute | solution.py:338
  58.2 5.1 %collective-permute-start.6 = (bf16[256,640]{1,0:T(8,128)(2,1)S(1)}, bf16[256,640]{1,0:T(8,128)(2,1)S(1)}, u32[]{:S(2)}, u32[]{:S(2)}) collective-permute-start(bf16[256,640]{1,0:T(8,128)(2,1)S(1)} %shard_map.99), channel_id=1, source_target_pairs={{0,8},{8,0},{4,12},{12,4},{1,9},{9,1},{5,13},{13,5},{2,10},{10,2},... | collective-permute-start | bytes 983048 | tf_op jit(solution)/shard_map/ppermute | solution.py:338
  63.3 2.5 %collective-permute-done.8.b_ref = bf16[192,640]{1,0:T(8,128)(2,1)S(1)} collective-permute-done((bf16[192,640]{1,0:T(8,128)(2,1)S(1)}, bf16[192,640]{1,0:T(8,128)(2,1)S(1)}, u32[]{:S(2)}, u32[]{:S(2)}) %collective-permute-start.8) | collective-permute-done | bytes 245792 | tf_op jit(solution)/shard_map/ppermute | solution.py:338
  65.8 0.1 shard_map.100
  65.8 4.0 %shard_map.101 = bf16[384,2560]{1,0:T(8,128)(2,1)} custom-call(bf16[256,384]{1,0:T(8,128)(2,1)S(1)} %get-tuple-element.75.lg_a, bf16[192,384]{1,0:T(8,128)(2,1)S(1)} %get-tuple-element.65.lg_b, bf16[448,640]{1,0:T(8,128)(2,1)S(1)} %get-tuple-element.53.own_ref.refs_0_, bf16[448,640]{1,0:T(8,128)(2,1)S(1)} %collective-permute-done.near_ref.refs_1_, ...), custom_call_target="tpu_custom_call" | custom-call | flops 880803840 | tf_op jit(solution)/shard_map/pallas_call | solution.py:117
  69.8 3.5 %collective-permute-done.7.refs_2_ = bf16[256,640]{1,0:T(8,128)(2,1)S(1)} collective-permute-done((bf16[256,640]{1,0:T(8,128)(2,1)S(1)}, bf16[256,640]{1,0:T(8,128)(2,1)S(1)}, u32[]{:S(2)}, u32[]{:S(2)}) %collective-permute-start.7) | collective-permute-done | bytes 327712 | tf_op jit(solution)/shard_map/ppermute | solution.py:338
  73.4 1.6 %collective-permute-done.6.refs_3_ = bf16[256,640]{1,0:T(8,128)(2,1)S(1)} collective-permute-done((bf16[256,640]{1,0:T(8,128)(2,1)S(1)}, bf16[256,640]{1,0:T(8,128)(2,1)S(1)}, u32[]{:S(2)}, u32[]{:S(2)}) %collective-permute-start.6) | collective-permute-done | bytes 327712 | tf_op jit(solution)/shard_map/ppermute | solution.py:338
  75.0 0.3 collective-permute-start.11
  75.3 2.4 %collective-permute-start.12 = (bf16[192,640]{1,0:T(8,128)(2,1)S(1)}, bf16[192,640]{1,0:T(8,128)(2,1)S(1)}, u32[]{:S(2)}, u32[]{:S(2)}) collective-permute-start(bf16[192,640]{1,0:T(8,128)(2,1)S(1)} %shard_map.100), channel_id=1, source_target_pairs={{0,8},{8,0},{4,12},{12,4},{1,9},{9,1},{5,13},{13,5},{2,10},{10,2},... | collective-permute-start | bytes 737288 | tf_op jit(solution)/shard_map/ppermute | solution.py:338
  77.7 0.6 shard_map.102
  78.3 1.6 %collective-permute-start.10 = (bf16[256,640]{1,0:T(8,128)(2,1)S(1)}, bf16[256,640]{1,0:T(8,128)(2,1)S(1)}, u32[]{:S(2)}, u32[]{:S(2)}) collective-permute-start(bf16[256,640]{1,0:T(8,128)(2,1)S(1)} %get-tuple-element.83), channel_id=1, source_target_pairs={{0,2},{2,0},{1,3},{3,1},{4,6},{6,4},{5,7},{7,5},{8,10},{10,8},{9,1... | collective-permute-start | bytes 983048 | tf_op jit(solution)/shard_map/ppermute | solution.py:30
  79.9 0.0 collective-permute-start.9
  79.9 2.5 %collective-permute-done.11.refs_2_ = bf16[192,640]{1,0:T(8,128)(2,1)S(1)} collective-permute-done((bf16[192,640]{1,0:T(8,128)(2,1)S(1)}, bf16[192,640]{1,0:T(8,128)(2,1)S(1)}, u32[]{:S(2)}, u32[]{:S(2)}) %collective-permute-start.11) | collective-permute-done | bytes 245792 | tf_op jit(solution)/shard_map/ppermute | solution.py:338
  82.3 1.8 %collective-permute-done.12.refs_3_ = bf16[192,640]{1,0:T(8,128)(2,1)S(1)} collective-permute-done((bf16[192,640]{1,0:T(8,128)(2,1)S(1)}, bf16[192,640]{1,0:T(8,128)(2,1)S(1)}, u32[]{:S(2)}, u32[]{:S(2)}) %collective-permute-start.12) | collective-permute-done | bytes 245792 | tf_op jit(solution)/shard_map/ppermute | solution.py:338
  84.2 0.8 shard_map.103
  84.9 1.6 %collective-permute-start.14 = (bf16[192,640]{1,0:T(8,128)(2,1)S(1)}, bf16[192,640]{1,0:T(8,128)(2,1)S(1)}, u32[]{:S(2)}, u32[]{:S(2)}) collective-permute-start(bf16[192,640]{1,0:T(8,128)(2,1)S(1)} %get-tuple-element.89), channel_id=1, source_target_pairs={{0,2},{2,0},{1,3},{3,1},{4,6},{6,4},{5,7},{7,5},{8,10},{10,8},{9,1... | collective-permute-start | bytes 737288 | tf_op jit(solution)/shard_map/ppermute | solution.py:30
  86.5 0.0 collective-permute-start.13
  86.5 1.1 %shard_map.106 = (f32[441,1,640]{2,1,0:T(1,128)}, f32[441,1,640]{2,1,0:T(1,128)}) custom-call(f32[256,640]{1,0:T(8,128)S(1)} %get-tuple-element.95.refs_0_, f32[256,640]{1,0:T(8,128)S(1)} %get-tuple-element.96.refs_1_), custom_call_target="tpu_custom_call" | custom-call | tf_op jit(solution)/shard_map/pallas_call | solution.py:117
  87.6 1.0 %shard_map.107 = (f32[441,1,640]{2,1,0:T(1,128)}, f32[441,1,640]{2,1,0:T(1,128)}) custom-call(f32[185,640]{1,0:T(8,128)S(1)} %get-tuple-element.93.refs_0_, f32[185,640]{1,0:T(8,128)S(1)} %get-tuple-element.94.refs_1_, f32[441,1,640]{2,1,0:T(1,128)} %get-tuple-element.97.refs_2_, ...), custom_call_target="tpu_custom_call", output_to_operand_aliasing={{0}: (2, {}), {1}: (3, {})} | custom-call | tf_op jit(solution)/shard_map/pallas_call | solution.py:117
  88.5 0.0 collective-permute-done.10.refs_3_
  88.5 0.0 collective-permute-done.9.refs_2_
  88.6 0.9 %shard_map.104.refs_4_ = f32[441,1,640]{2,1,0:T(1,128)} custom-call(s32[1]{0:T(128)S(6)} %copy.16._.refs_0_, f32[256,640]{1,0:T(8,128)S(1)} %get-tuple-element.90.refs_1_, bf16[256,640]{1,0:T(8,128)(2,1)S(1)} %collective-permute-done.9.refs_2_, bf16[256,640]{1,0:T(8,128)(2,1)S(1)} %collective-permute-done.10.refs_3_), custom_call_target="tpu_custom_call" | custom-call | tf_op jit(solution)/shard_map/pallas_call | solution.py:117
  89.5 1.7 %collective-permute-done.14.refs_3_ = bf16[192,640]{1,0:T(8,128)(2,1)S(1)} collective-permute-done((bf16[192,640]{1,0:T(8,128)(2,1)S(1)}, bf16[192,640]{1,0:T(8,128)(2,1)S(1)}, u32[]{:S(2)}, u32[]{:S(2)}) %collective-permute-start.14) | collective-permute-done | bytes 245792 | tf_op jit(solution)/shard_map/ppermute | solution.py:30
  91.2 0.0 collective-permute-done.13.refs_2_
  91.2 0.8 shard_map.105
Async XLA Ops:
  0.6 1.3 %copy-start.1 = (f32[1,640,441]{1,0,2:T(1,128)S(1)}, f32[1,640,441]{1,0,2:T(1,128)}, u32[]{:S(2)}) copy-start(f32[1,640,441]{1,0,2:T(1,128)} %param.8) | copy-start | bytes 3386884
  1.9 7.6 %copy-start.2 = (f32[1,640,441]{1,0,2:T(1,128)S(1)}, f32[1,640,441]{1,0,2:T(1,128)}, u32[]{:S(2)}) copy-start(f32[1,640,441]{1,0,2:T(1,128)} %param.8) | copy-start | bytes 3386884
  2.8 19.8 %collective-permute-start.1 = (bf16[256,640]{1,0:T(8,128)(2,1)S(1)}, bf16[256,640]{1,0:T(8,128)(2,1)S(1)}, u32[]{:S(2)}, u32[]{:S(2)}) collective-permute-start(bf16[256,640]{1,0:T(8,128)(2,1)S(1)} %get-tuple-element.54), channel_id=1, source_target_pairs={{0,8},{8,0},{4,12},{12,4},{1,9},{9,1},{5,13},{13,5},{2,10},{10,2},... | collective-permute-start | bytes 983048 | tf_op jit(solution)/shard_map/ppermute | solution.py:338
  6.9 28.0 %collective-permute-start = (bf16[448,640]{1,0:T(8,128)(2,1)S(1)}, bf16[448,640]{1,0:T(8,128)(2,1)S(1)}, u32[]{:S(2)}, u32[]{:S(2)}) collective-permute-start(bf16[448,640]{1,0:T(8,128)(2,1)S(1)} %get-tuple-element.53.own_ref.refs_0_), channel_id=1, source_target_pairs={{0,4},{4,0},{8,12},{12,8},{1,5},{5,1},{9,13},{13,9},{2,6},{6,2},{1... | collective-permute-start | bytes 1720328 | tf_op jit(solution)/shard_map/ppermute | solution.py:338
  8.5 24.1 %collective-permute-start.3 = (bf16[192,640]{1,0:T(8,128)(2,1)S(1)}, bf16[192,640]{1,0:T(8,128)(2,1)S(1)}, u32[]{:S(2)}, u32[]{:S(2)}) collective-permute-start(bf16[192,640]{1,0:T(8,128)(2,1)S(1)} %get-tuple-element.60), channel_id=1, source_target_pairs={{0,8},{8,0},{4,12},{12,4},{1,9},{9,1},{5,13},{13,5},{2,10},{10,2},... | collective-permute-start | bytes 737288 | tf_op jit(solution)/shard_map/ppermute | solution.py:338
  9.5 1.3 %copy-start.3 = (f32[1,640,441]{1,0,2:T(1,128)S(1)}, f32[1,640,441]{1,0,2:T(1,128)}, u32[]{:S(2)}) copy-start(f32[1,640,441]{1,0,2:T(1,128)} %param.9) | copy-start | bytes 3386884
  10.7 1.3 %copy-start.4 = (f32[1,640,441]{1,0,2:T(1,128)S(1)}, f32[1,640,441]{1,0,2:T(1,128)}, u32[]{:S(2)}) copy-start(f32[1,640,441]{1,0,2:T(1,128)} %param.10) | copy-start | bytes 3386884
  12.0 2.3 %copy-start = (bf16[1,384,2560]{2,1,0:T(8,128)(2,1)S(1)}, bf16[1,384,2560]{2,1,0:T(8,128)(2,1)}, u32[]{:S(2)}) copy-start(bf16[1,384,2560]{2,1,0:T(8,128)(2,1)} %param.6) | copy-start | bytes 5898244
  22.6 22.2 %copy-start.5 = (s32[1,384]{1,0:T(1,128)S(1)}, s32[1,384]{1,0:T(1,128)}, u32[]{:S(2)}) copy-start(s32[1,384]{1,0:T(1,128)} %refs_4_.1) | copy-start | bytes 4612
  22.6 18.4 %collective-permute-start.2 = (bf16[256,640]{1,0:T(8,128)(2,1)S(1)}, bf16[256,640]{1,0:T(8,128)(2,1)S(1)}, u32[]{:S(2)}, u32[]{:S(2)}) collective-permute-start(bf16[256,640]{1,0:T(8,128)(2,1)S(1)} %collective-permute-done.1.far_a.refs_2_), channel_id=1, source_target_pairs={{0,4},{4,0},{8,12},{12,8},{1,5},{5,1},{9,13},{13,9},{2,6},{6,2},{1... | collective-permute-start | bytes 983048 | tf_op jit(solution)/shard_map/ppermute | solution.py:338
  32.6 12.1 %collective-permute-start.4 = (bf16[192,640]{1,0:T(8,128)(2,1)S(1)}, bf16[192,640]{1,0:T(8,128)(2,1)S(1)}, u32[]{:S(2)}, u32[]{:S(2)}) collective-permute-start(bf16[192,640]{1,0:T(8,128)(2,1)S(1)} %collective-permute-done.3.far_b.refs_4_), channel_id=1, source_target_pairs={{0,4},{4,0},{8,12},{12,8},{1,5},{5,1},{9,13},{13,9},{2,6},{6,2},{1... | collective-permute-start | bytes 737288 | tf_op jit(solution)/shard_map/ppermute | solution.py:338
  45.8 10.7 %collective-permute-start.5 = (bf16[256,640]{1,0:T(8,128)(2,1)S(1)}, bf16[256,640]{1,0:T(8,128)(2,1)S(1)}, u32[]{:S(2)}, u32[]{:S(2)}) collective-permute-start(bf16[256,640]{1,0:T(8,128)(2,1)S(1)} %get-tuple-element.68), channel_id=1, source_target_pairs={{0,4},{4,0},{8,12},{12,8},{1,5},{5,1},{9,13},{13,9},{2,6},{6,2},{1... | collective-permute-start | bytes 983048 | tf_op jit(solution)/shard_map/ppermute | solution.py:338
  47.4 18.4 %collective-permute-start.8 = (bf16[192,640]{1,0:T(8,128)(2,1)S(1)}, bf16[192,640]{1,0:T(8,128)(2,1)S(1)}, u32[]{:S(2)}, u32[]{:S(2)}) collective-permute-start(bf16[192,640]{1,0:T(8,128)(2,1)S(1)} %get-tuple-element.72), channel_id=1, source_target_pairs={{0,4},{4,0},{8,12},{12,8},{1,5},{5,1},{9,13},{13,9},{2,6},{6,2},{1... | collective-permute-start | bytes 737288 | tf_op jit(solution)/shard_map/ppermute | solution.py:338
  56.6 16.8 %collective-permute-start.7 = (bf16[256,640]{1,0:T(8,128)(2,1)S(1)}, bf16[256,640]{1,0:T(8,128)(2,1)S(1)}, u32[]{:S(2)}, u32[]{:S(2)}) collective-permute-start(bf16[256,640]{1,0:T(8,128)(2,1)S(1)} %get-tuple-element.70), channel_id=1, source_target_pairs={{0,4},{4,0},{8,12},{12,8},{1,5},{5,1},{9,13},{13,9},{2,6},{6,2},{1... | collective-permute-start | bytes 983048 | tf_op jit(solution)/shard_map/ppermute | solution.py:338
  58.2 16.8 %collective-permute-start.6 = (bf16[256,640]{1,0:T(8,128)(2,1)S(1)}, bf16[256,640]{1,0:T(8,128)(2,1)S(1)}, u32[]{:S(2)}, u32[]{:S(2)}) collective-permute-start(bf16[256,640]{1,0:T(8,128)(2,1)S(1)} %shard_map.99), channel_id=1, source_target_pairs={{0,8},{8,0},{4,12},{12,4},{1,9},{9,1},{5,13},{13,5},{2,10},{10,2},... | collective-permute-start | bytes 983048 | tf_op jit(solution)/shard_map/ppermute | solution.py:338
  75.0 7.4 %collective-permute-start.11 = (bf16[192,640]{1,0:T(8,128)(2,1)S(1)}, bf16[192,640]{1,0:T(8,128)(2,1)S(1)}, u32[]{:S(2)}, u32[]{:S(2)}) collective-permute-start(bf16[192,640]{1,0:T(8,128)(2,1)S(1)} %get-tuple-element.85), channel_id=1, source_target_pairs={{0,4},{4,0},{8,12},{12,8},{1,5},{5,1},{9,13},{13,9},{2,6},{6,2},{1... | collective-permute-start | bytes 737288 | tf_op jit(solution)/shard_map/ppermute | solution.py:338
  75.3 8.9 %collective-permute-start.12 = (bf16[192,640]{1,0:T(8,128)(2,1)S(1)}, bf16[192,640]{1,0:T(8,128)(2,1)S(1)}, u32[]{:S(2)}, u32[]{:S(2)}) collective-permute-start(bf16[192,640]{1,0:T(8,128)(2,1)S(1)} %shard_map.100), channel_id=1, source_target_pairs={{0,8},{8,0},{4,12},{12,4},{1,9},{9,1},{5,13},{13,5},{2,10},{10,2},... | collective-permute-start | bytes 737288 | tf_op jit(solution)/shard_map/ppermute | solution.py:338
  78.3 10.2 %collective-permute-start.10 = (bf16[256,640]{1,0:T(8,128)(2,1)S(1)}, bf16[256,640]{1,0:T(8,128)(2,1)S(1)}, u32[]{:S(2)}, u32[]{:S(2)}) collective-permute-start(bf16[256,640]{1,0:T(8,128)(2,1)S(1)} %get-tuple-element.83), channel_id=1, source_target_pairs={{0,2},{2,0},{1,3},{3,1},{4,6},{6,4},{5,7},{7,5},{8,10},{10,8},{9,1... | collective-permute-start | bytes 983048 | tf_op jit(solution)/shard_map/ppermute | solution.py:30
  79.9 8.7 %collective-permute-start.9 = (bf16[256,640]{1,0:T(8,128)(2,1)S(1)}, bf16[256,640]{1,0:T(8,128)(2,1)S(1)}, u32[]{:S(2)}, u32[]{:S(2)}) collective-permute-start(bf16[256,640]{1,0:T(8,128)(2,1)S(1)} %get-tuple-element.83), channel_id=1, source_target_pairs={{0,1},{1,0},{2,3},{3,2},{4,5},{5,4},{6,7},{7,6},{8,9},{9,8},{10,11... | collective-permute-start | bytes 983048 | tf_op jit(solution)/shard_map/ppermute | solution.py:30
  84.9 6.3 %collective-permute-start.14 = (bf16[192,640]{1,0:T(8,128)(2,1)S(1)}, bf16[192,640]{1,0:T(8,128)(2,1)S(1)}, u32[]{:S(2)}, u32[]{:S(2)}) collective-permute-start(bf16[192,640]{1,0:T(8,128)(2,1)S(1)} %get-tuple-element.89), channel_id=1, source_target_pairs={{0,2},{2,0},{1,3},{3,1},{4,6},{6,4},{5,7},{7,5},{8,10},{10,8},{9,1... | collective-permute-start | bytes 737288 | tf_op jit(solution)/shard_map/ppermute | solution.py:30
  86.5 4.7 %collective-permute-start.13 = (bf16[192,640]{1,0:T(8,128)(2,1)S(1)}, bf16[192,640]{1,0:T(8,128)(2,1)S(1)}, u32[]{:S(2)}, u32[]{:S(2)}) collective-permute-start(bf16[192,640]{1,0:T(8,128)(2,1)S(1)} %get-tuple-element.89), channel_id=1, source_target_pairs={{0,1},{1,0},{2,3},{3,2},{4,5},{5,4},{6,7},{7,6},{8,9},{9,8},{10,11... | collective-permute-start | bytes 737288 | tf_op jit(solution)/shard_map/ppermute | solution.py:30
